TPU v7x, 256 devices: a whole 4x4x8 slice. The times are simulated.
256 devices in a mesh: dp: 8 (over z), ctx: 32 (over x, y, core).
Axes of the slice: x: 4, y: 4, z: 8, core: 2. Of those that a mesh axis runs over, the one named last changes fastest.
Arguments:
- conv_input: bfloat16 [8, 4096, 2816], P('dp', 'ctx'), may hold values from -6 to 6
- step_raw: float32 [8, 4096, 40], P('dp', 'ctx'), may hold values from -13 to -3
- log_decay: float32 [8, 4096, 40], P('dp', 'ctx'), may hold values from -1 to 0
- cotangent: bfloat16 [8, 4096, 2560], P('dp', 'ctx'), may hold values from -24 to 24
- conv_weight: float32 [4, 2816], replicated, may hold values from -3 to 3
- conv_bias: float32 [2816], replicated, may hold values from -0.5 to 0.5
- skip_gain: float32 [40], replicated, may hold values from 0.5 to 1.5
Outputs:
- layer_output: bfloat16 [8, 4096, 2560], P('dp', 'ctx')
- input_grad: bfloat16 [8, 4096, 2816], P('dp', 'ctx')
- step_grad: float32 [8, 4096, 40], P('dp', 'ctx')
- weight_grad: float32 [4, 2816], replicated
- bias_grad: float32 [2816], replicated
- skip_grad: float32 [40], replicated
All inputs are finite; a program needn't handle non-finite values.
Results may differ from a plain program's by a relative error of at most 0.014.
Values may be sent and summed in bfloat16 or wider, within the bound.
A program may use at most 192 MiB of HBM per device.

v0:
```python
import jax
import jax.numpy as jnp
from jax import lax
from jax.sharding import PartitionSpec as P

ATTENTION_LANES = 40
P_SIZE = 64
N = 128
K = 4


def passed_along(value, axis, steps):
    count = lax.axis_size(axis)
    leading, last = (max(0, -steps), min(count, count - steps))
    return lax.ppermute(value, axis, [(source, source + steps) for source in range(leading, last)])


def entering(part, axis, combine, identity, reverse):
    count = lax.axis_size(axis)
    place = lax.axis_index(axis)
    ahead = count - 1 - place if reverse else place
    gathered = jax.tree.map(lambda a: lax.all_gather(a, axis), part)
    state = jax.tree.map(lambda a, e: jnp.zeros_like(a) + jnp.asarray(e, a.dtype), part, identity)

    def one(step, state):
        source = count - 1 - step if reverse else step
        return combine(
            state, jax.tree.map(lambda a: lax.dynamic_index_in_dim(a, source, 0, False), gathered)
        )

    return lax.fori_loop(0, ahead, one, state)


def join_pairs(earlier, latter):
    return (earlier[0] * latter[0], latter[0][:, None, None] * earlier[1] + latter[1])


def heads_per_turn(lanes, length):
    chosen = 1
    for candidate in range(1, lanes + 1):
        if lanes % candidate == 0 and candidate * length * length <= 4194304:
            chosen = candidate
    return chosen


def body(conv_input, step_raw, log_decay, cotangent, conv_weight, conv_bias, skip_gain):
    series = conv_input[0]
    length, channels = series.shape
    halo_rows = passed_along(series[length - (K - 1) :], "ctx", 1)
    extended = jnp.concatenate([halo_rows, series], axis=0).astype(jnp.float32)
    before = jnp.zeros((length, channels), jnp.float32) + conv_bias[None, :]
    for offset in range(K):
        before = before + conv_weight[offset][None, :] * extended[offset : offset + length]
    activated = jax.nn.silu(before).astype(jnp.bfloat16)
    signal = activated[:, : ATTENTION_LANES * P_SIZE].reshape(length, ATTENTION_LANES, P_SIZE)
    inject = activated[:, ATTENTION_LANES * P_SIZE : ATTENTION_LANES * P_SIZE + N]
    readout = activated[:, ATTENTION_LANES * P_SIZE + N :]
    raw_steps = step_raw[0]
    step_size = jax.nn.softplus(raw_steps)
    positions = jnp.arange(length, dtype=jnp.int32)
    causal = positions[:, None] >= positions[None, :]
    lower_ones = causal.astype(jnp.float32)
    decay_sum = jnp.dot(lower_ones, log_decay[0], precision=lax.Precision.HIGHEST)
    decay_end = decay_sum[length - 1]
    block_decay = jnp.exp(decay_end)
    to_end = jnp.exp(decay_end[None, :] - decay_sum)
    from_start = jnp.exp(decay_sum)
    grad_heads = cotangent[0].reshape(length, ATTENTION_LANES, P_SIZE)
    signal_tail = (signal.astype(jnp.float32) * (step_size * to_end)[:, :, None]).astype(
        jnp.bfloat16
    )
    grad_start = (grad_heads.astype(jnp.float32) * from_start[:, :, None]).astype(jnp.bfloat16)
    signal_step = (signal.astype(jnp.float32) * step_size[:, :, None]).astype(jnp.bfloat16)
    local_state = jnp.einsum("lhp,ln->hpn", signal_tail, inject, preferred_element_type=jnp.float32)
    local_adjoint = jnp.einsum(
        "lhp,ln->hpn", grad_start, readout, preferred_element_type=jnp.float32
    )
    unit_decay = jnp.ones((ATTENTION_LANES,), jnp.float32)
    zero_state = jnp.zeros((ATTENTION_LANES, P_SIZE, N), jnp.float32)
    incoming = entering(
        (block_decay, local_state), "ctx", join_pairs, (unit_decay, zero_state), False
    )[1]
    adjoint = entering(
        (block_decay, local_adjoint), "ctx", join_pairs, (unit_decay, zero_state), True
    )[1]
    scores = jnp.dot(readout, inject.T, preferred_element_type=jnp.float32)
    per_turn = heads_per_turn(ATTENTION_LANES, length)
    groups = ATTENTION_LANES // per_turn
    sum_groups = decay_sum.T.reshape(groups, per_turn, length)
    step_groups = step_size.T.reshape(groups, per_turn, length)
    signal_groups = signal.reshape(length, groups, per_turn, P_SIZE).transpose(1, 0, 2, 3)
    scaled_groups = signal_step.reshape(length, groups, per_turn, P_SIZE).transpose(1, 0, 2, 3)
    grad_groups = grad_heads.reshape(length, groups, per_turn, P_SIZE).transpose(1, 0, 2, 3)
    sum_group = sum_groups[0]
    step_group = step_groups[0]
    signal_group = signal_groups[0]
    scaled_group = scaled_groups[0]
    grad_group = grad_groups[0]
    log_gap = jnp.where(causal[None], sum_group[:, :, None] - sum_group[:, None, :], -1e30)
    fading = jnp.exp(log_gap)
    mixing = (fading * scores[None]).astype(jnp.bfloat16)
    out_part = jnp.einsum("hts,shp->thp", mixing, scaled_group, preferred_element_type=jnp.float32)
    back_part = jnp.einsum("hts,thp->shp", mixing, grad_group, preferred_element_type=jnp.float32)
    inner_prod = jnp.einsum(
        "thp,shp->hts", grad_group, signal_group, preferred_element_type=jnp.float32
    )
    weighted = fading * step_group[:, None, :]
    running = jnp.sum(weighted * inner_prod, axis=0)
    single_outs = (out_part, back_part)
    out_intra = single_outs[0]
    back_intra = single_outs[1]
    mix_total = running.astype(jnp.bfloat16)
    incoming_b = incoming.astype(jnp.bfloat16)
    adjoint_b = adjoint.astype(jnp.bfloat16)
    out_full = (
        out_intra
        + from_start[:, :, None]
        * jnp.einsum("ln,hpn->lhp", readout, incoming_b, preferred_element_type=jnp.float32)
        + skip_gain[None, :, None] * signal.astype(jnp.float32)
    )
    back_full = back_intra + to_end[:, :, None] * jnp.einsum(
        "ln,hpn->lhp", inject, adjoint_b, preferred_element_type=jnp.float32
    )
    grad_signal = step_size[:, :, None] * back_full + skip_gain[None, :, None] * grad_heads.astype(
        jnp.float32
    )
    step_part = jnp.sum(signal.astype(jnp.float32) * back_full, axis=2) * jax.nn.sigmoid(raw_steps)
    grad_readout = jnp.dot(mix_total, inject, preferred_element_type=jnp.float32) + jnp.einsum(
        "lhp,hpn->ln", grad_start, incoming_b, preferred_element_type=jnp.float32
    )
    grad_inject = jnp.dot(mix_total.T, readout, preferred_element_type=jnp.float32) + jnp.einsum(
        "lhp,hpn->ln", signal_tail, adjoint_b, preferred_element_type=jnp.float32
    )
    grad_act = jnp.concatenate(
        [grad_signal.reshape(length, ATTENTION_LANES * P_SIZE), grad_inject, grad_readout], axis=1
    )
    sigmoid_pre = jax.nn.sigmoid(before)
    grad_pre = grad_act * sigmoid_pre * (1.0 + before * (1.0 - sigmoid_pre))
    after_rows = passed_along(grad_pre[: K - 1], "ctx", -1)
    padded_grad = jnp.concatenate([grad_pre, after_rows], axis=0)
    grad_in = jnp.zeros((length, channels), jnp.float32)
    for offset in range(K):
        grad_in = (
            grad_in
            + conv_weight[offset][None, :] * padded_grad[K - 1 - offset : K - 1 - offset + length]
        )
    weight_part = jnp.stack(
        [jnp.sum(grad_pre * extended[offset : offset + length], axis=0) for offset in range(K)]
    )
    bias_part = jnp.sum(grad_pre, axis=0)
    skip_part = jnp.sum(grad_heads.astype(jnp.float32) * signal.astype(jnp.float32), axis=(0, 2))
    weight_grad, bias_grad, skip_grad = lax.psum((weight_part, bias_part, skip_part), ("dp", "ctx"))
    layer_output = out_full.reshape(1, length, ATTENTION_LANES * P_SIZE).astype(jnp.bfloat16)
    input_grad = grad_in.reshape(1, length, channels).astype(jnp.bfloat16)
    step_grad = step_part.reshape(1, length, ATTENTION_LANES)
    return (layer_output, input_grad, step_grad, weight_grad, bias_grad, skip_grad)


def solution(mesh):
    in_specs = (
        P("dp", "ctx", None),
        P("dp", "ctx", None),
        P("dp", "ctx", None),
        P("dp", "ctx", None),
        P(),
        P(),
        P(),
    )
    out_specs = (P("dp", "ctx", None), P("dp", "ctx", None), P("dp", "ctx", None), P(), P(), P())
    return jax.shard_map(body, mesh=mesh, in_specs=in_specs, out_specs=out_specs, check_vma=False)
```

profile of v0, /device:TPU:1, one launch (start us, length us, event | category | flops | bytes accessed | tf_op | source)
XLA Modules:
  0.0 481.7 jit_solution(5900088018161955126)
XLA Ops:
  8.0 4.6 collective-permute-start
  16.8 2.0 multiply_convert_fusion.1
  22.7 2.2 copy.49
  24.8 2.5 fusion.38
  27.4 23.5 %all-gather.2 = f32[32,1,40]{2,1,0:T(1,128)} all-gather(f32[1,1,40]{2,1,0:T(1,128)S(1)} %bitcast.113), channel_id=1, replica_groups=mesh['dp'=8,'ctx'=32] {'ctx'}, dimensions={0}, use_global_device_ids=true | all-gather | bytes 5280 | tf_op jit(solution)/shard_map/all_gather | solution.py:22
  53.2 3.5 fusion
  56.7 109.3 %all-gather.6.cloned.1.call-done = f32[1280,64,128]{2,1,0:T(8,128)} async-done(((f32[40,64,128]{2,1,0:T(8,128)}), f32[1280,64,128]{2,1,0:T(8,128)}) %all-gather.6.cloned.1.call-update) | async-done | bytes 41943056 | tf_op jit(solution)/shard_map/all_gather | solution.py:22
  166.1 2.3 while.26
  166.8 1.6 bitcast_add_fusion.4
  168.4 2.1 convolution_bitcast_fusion.2
  170.5 2.2 convolution_multiply_fusion.1
  172.7 135.8 %all-gather.8.cloned.1.call-done = f32[1280,64,128]{2,1,0:T(8,128)} async-done(((f32[40,64,128]{2,1,0:T(8,128)}), f32[1280,64,128]{2,1,0:T(8,128)}) %all-gather.8.cloned.1.call-update) | async-done | bytes 41943056 | tf_op jit(solution)/shard_map/all_gather | solution.py:22
  308.6 68.6 %while.27 = (s32[]{:T(128)}, f32[40,64,128]{2,1,0:T(8,128)S(1)}, s32[]{:T(128)}, f32[32,40]{1,0:T(8,128)}, f32[32,40,64,128]{3,2,1,0:T(8,128)}, /*index=5*/s32[]{:T(128)}, s32[]{:T(128)}, s32[]{:T(128)}, s32[]{:T(128)}) while((s32[]{:T(128)}, f32[40,64,128]{2,1,0:T(8,128)S(1)}, s32[]{:T(128)}, f32[32,40]{1,0:T(8,128)}, ...), condition=%wide.region_3.4_spmd, body=%wide.region_2.3_spmd.sunk | while | flops 655366 | bytes 3932795 | solution.py:31
  309.3 1.6 bitcast_add_fusion.5
  311.6 1.6 bitcast_add_fusion.5
  313.9 1.6 bitcast_add_fusion.5
  316.2 1.6 bitcast_add_fusion.5
  318.5 1.6 bitcast_add_fusion.5
  320.8 1.6 bitcast_add_fusion.5
  323.0 1.6 bitcast_add_fusion.5
  325.3 1.6 bitcast_add_fusion.5
  327.6 1.6 bitcast_add_fusion.5
  329.9 1.6 bitcast_add_fusion.5
  332.2 1.6 bitcast_add_fusion.5
  334.5 1.6 bitcast_add_fusion.5
  336.7 1.6 bitcast_add_fusion.5
  339.0 1.6 bitcast_add_fusion.5
  341.3 1.6 bitcast_add_fusion.5
  343.6 1.6 bitcast_add_fusion.5
  345.9 1.6 bitcast_add_fusion.5
  348.2 1.6 bitcast_add_fusion.5
  350.5 1.6 bitcast_add_fusion.5
  352.8 1.6 bitcast_add_fusion.5
  355.1 1.6 bitcast_add_fusion.5
  357.4 1.6 bitcast_add_fusion.5
  359.7 1.6 bitcast_add_fusion.5
  362.0 1.6 bitcast_add_fusion.5
  366.5 1.6 bitcast_add_fusion.5
  368.8 1.6 bitcast_add_fusion.5
  373.4 1.6 bitcast_add_fusion.5
  375.7 1.6 bitcast_add_fusion.5
  379.7 1.6 convolution_add_fusion.1
  382.5 2.1 fusion.14
  384.6 1.8 fusion.19
  387.9 3.1 multiply_reduce_fusion.3
  391.0 4.4 collective-permute-start.1
  396.2 2.2 copy.56
  398.4 74.9 %all-reduce = (f32[4,2816]{1,0:T(4,128)}, f32[2816]{0:T(1024)}, f32[40]{0:T(128)}) all-reduce(f32[4,2816]{1,0:T(4,128)S(1)} %pad_maximum_fusion.1, f32[2816]{0:T(1024)S(1)} %get-tuple-element.164, f32[40]{0:T(128)S(1)} %reduce_sum.91), channel_id=1, replica_groups=mesh['dp'=8,'ctx'=32] {'dp','ctx'}, use_global_device_ids=true, to_apply=%region_10.11 | all-reduce | flops 14120 | bytes 112960 | tf_op jit(solution)/shard_map/psum | solution.py:152
  (115 shorter events, 43.0 us)
Async XLA Ops:
  7.2 5.5 %copy-start = (f32[1,128,40]{1,2,0:T(8,128)S(1)}, f32[1,128,40]{1,2,0:T(8,128)}, u32[]{:S(2)}) copy-start(f32[1,128,40]{1,2,0:T(8,128)} %param.13) | copy-start | bytes 61444
  7.2 9.7 %copy-start.22 = (f32[2816]{0:T(1024)S(1)}, f32[2816]{0:T(1024)}, u32[]{:S(2)}) copy-start(f32[2816]{0:T(1024)} %param.16) | copy-start | bytes 33796
  7.2 158.8 %all-gather.6.cloned.1.call-start = ((), (), s32[]{:S(2)}) async-start(), calls=%async_computation | async-start | bytes 43253760 | tf_op jit(solution)/shard_map/all_gather | solution.py:22
  8.0 7.5 %collective-permute-start = (bf16[3,2816]{1,0:T(4,128)(2,1)S(1)}, bf16[3,2816]{1,0:T(4,128)(2,1)S(1)}, u32[]{:S(2)}, u32[]{:S(2)}) collective-permute-start(bf16[3,2816]{1,0:T(4,128)(2,1)S(1)} %slice_bitcast_fusion), channel_id=1, source_target_pairs={{0,1},{1,2},{2,3},{3,4},{4,5},{5,6},{6,7},{7,8},{8,9},{9,10},{10,1... | collective-permute-start | bytes 50696 | tf_op jit(solution)/shard_map/ppermute | solution.py:15
  12.8 40.3 %copy-start.6 = (f32[128,40]{0,1:T(8,128)}, f32[128,40]{0,1:T(8,128)S(1)}, u32[]{:S(2)}) copy-start(f32[128,40]{0,1:T(8,128)S(1)} %fusion.57) | copy-start | bytes 61444
  15.5 3.3 copy-start.9
  15.5 3.3 copy-start.11
  15.5 3.3 copy-start.13
  18.9 33.5 %copy-start.2 = (bf16[128,2816]{1,0:T(8,128)(2,1)}, bf16[128,2816]{1,0:T(8,128)(2,1)S(1)}, u32[]{:S(2)}) copy-start(bf16[128,2816]{1,0:T(8,128)(2,1)S(1)} %get-tuple-element.197) | copy-start | bytes 2162692
  22.6 285.9 %all-gather.8.cloned.1.call-start = ((), (), s32[]{:S(2)}) async-start(), calls=%async_computation.1 | async-start | bytes 43253760 | tf_op jit(solution)/shard_map/all_gather | solution.py:22
  50.9 5.8 %copy-start.20 = (pred[128,128]{0,1:T(8,128)(4,1)}, pred[128,128]{0,1:T(8,128)(4,1)S(1)}, u32[]{:S(2)}) copy-start(pred[128,128]{0,1:T(8,128)(4,1)S(1)} %iota_compare_fusion) | copy-start | bytes 49156
  377.3 0.8 copy-start.5
  377.3 0.8 copy-start.8
  377.3 4.0 copy-start.15
  379.7 2.7 copy-start.4
  379.7 2.8 copy-start.7
  379.7 2.8 copy-start.17
  379.7 2.8 copy-start.18
  379.7 2.8 copy-start.21
  379.7 2.8 copy-start.23
  382.5 2.1 copy-start.3
  387.9 7.7 %copy-start.16 = (f32[1,128,40]{1,2,0:T(8,128)S(1)}, f32[1,128,40]{1,2,0:T(8,128)}, u32[]{:S(2)}) copy-start(f32[1,128,40]{1,2,0:T(8,128)} %param.12) | copy-start | bytes 61444
  387.9 7.7 %copy-start.19 = (f32[128,40]{0,1:T(8,128)S(1)}, f32[128,40]{0,1:T(8,128)}, u32[]{:S(2)}) copy-start(f32[128,40]{0,1:T(8,128)} %get-tuple-element.199) | copy-start | bytes 61444
  391.0 82.3 %copy-start.10 = (f32[2816]{0:T(1024)S(1)}, f32[2816]{0:T(1024)}, u32[]{:S(2)}) copy-start(f32[2816]{0:T(1024)} %copy-done.9) | copy-start | bytes 33796
  391.0 82.3 %copy-start.12 = (f32[2816]{0:T(1024)S(1)}, f32[2816]{0:T(1024)}, u32[]{:S(2)}) copy-start(f32[2816]{0:T(1024)} %copy-done.11) | copy-start | bytes 33796
  391.0 82.3 %copy-start.14 = (f32[2816]{0:T(1024)S(1)}, f32[2816]{0:T(1024)}, u32[]{:S(2)}) copy-start(f32[2816]{0:T(1024)} %copy-done.13) | copy-start | bytes 33796
  391.0 82.3 %collective-permute-start.1 = (f32[3,2816]{1,0:T(4,128)S(1)}, f32[3,2816]{1,0:T(4,128)S(1)}, u32[]{:S(2)}, u32[]{:S(2)}) collective-permute-start(f32[3,2816]{1,0:T(4,128)S(1)} %slice.88), channel_id=1, source_target_pairs={{1,0},{2,1},{3,2},{4,3},{5,4},{6,5},{7,6},{8,7},{9,8},{10,9},{11,1... | collective-permute-start | bytes 101384 | tf_op jit(solution)/shard_map/ppermute | solution.py:15
  396.2 78.6 %copy-start.1 = (f32[1,128,40]{1,2,0:T(8,128)S(1)}, f32[1,128,40]{1,2,0:T(8,128)}, u32[]{:S(2)}) copy-start(f32[1,128,40]{1,2,0:T(8,128)} %param.13) | copy-start | bytes 61444
Sparse Core Ops, SparseCore 0:
  22.8 143.1 all-gather.5
  168.5 139.9 all-gather.7
where the time goes:
time: 485 us; the launch traced here: 482 us
  waiting for transfers between devices  245 us (51%)
  blocking collectives  98.4 us (20%)
  other arithmetic  60.2 us (12%)
  local copies, waits for them, and re-layouts  32.4 us (7%)
  matrix products  21.2 us (4%)
  between operations  14.4 us (3%)
  starting transfers between devices  9.12 us (2%)
    all_gather x2, waiting for transfers between devices, entering(): gathered = jax.tree.map(lambda a: lax.all_gather(a, axis), part)  245 us
    psum x1, blocking collectives, body(): lax.psum((weight_part, bias_part, skip_part), ('dp', 'ctx'))  74.9 us
    add x31, other arithmetic, join_pairs(): latter[0][:, None, None] * earlier[1] + latter[1]  48.8 us
    all_gather x1, blocking collectives, entering(): gathered = jax.tree.map(lambda a: lax.all_gather(a, axis), part)  23.5 us
    mul x31, local copies, waits for them, and re-layouts, join_pairs(): latter[0][:, None, None] * earlier[1] + latter[1]  21.3 us
  transfers between devices with their start and end apart: 4, of which 2 were waited for; matrix products, arithmetic and copies ran while one was open for 5% of the time, Pallas kernels for 0%

commit v1 on v0

v1 whole, which is shorter than its diff:
```python
import jax
import jax.numpy as jnp
from jax import lax
from jax.experimental import pallas as pl
from jax.experimental.pallas import tpu as pltpu
from jax.sharding import PartitionSpec as P

HEADS = 40
WIDTH = 64
STATE = 128
TAPS = 4
TOK = 128
SIG = HEADS * WIDTH
CH = SIG + 2 * STATE
BLOCKS = SIG // 128
CTX = 32
CHIPS = 16
DPS = 8
GROUPS = 4
GW = SIG // GROUPS
GB = GW // 128
HALF = STATE // 2
ROWS = 16
OWNERS = CH // 128
SPLIT = 10
LOG2E = 1.4426950408889634
F32 = jnp.float32
BF16 = jnp.bfloat16
MESH = pl.DeviceIdType.MESH


def dot(a, b, dims=((1,), (0,)), **kw):
    return lax.dot_general(a, b, (dims, ((), ())), preferred_element_type=F32, **kw)


def split3(v):
    hi = v.astype(BF16)
    rest = v - hi.astype(F32)
    mid = rest.astype(BF16)
    low = (rest - mid.astype(F32)).astype(BF16)
    return hi, mid, low


def loop(lo, hi, fn):
    def step(i, carry):
        fn(i)
        return carry

    lax.fori_loop(lo, hi, step, 0)


def cols(i, width=128):
    return pl.ds(pl.multiple_of(i * width, 128), width)


def kernel(
    x_ref, raw_ref, ld_ref, cot_ref, w_ref, b_ref, skip_ref,
    out_ref, gin_ref, sg_ref, wg_ref, bg_ref, kg_ref,
    xe, halo, act, dsil, ldp, dst, dsx, stx, fsx, tex, tail, gst, sst,
    loc, prt, dec, decp, decg, dcx, coef, skx, tsum, rcv, res, inc, snd, fin,
    oi, bi, run, gp, zhi, zlo, onehot, skp, part, ar1, ar2, sum1, tot,
    h_sem, d_sem, dg_s, dg_r, p1_s, p1_r, a_s, a_r, b_s, b_r, p2_s, p2_r, g_sem,
    r1_s, r1_r, r2_s, r2_r, r3_s, r3_r,
):
    me = lax.axis_index("ctx")
    zed = lax.axis_index("dp")
    core = lax.rem(me, 2)
    chip = me // 2
    quarter = lax.rem(chip, 4)
    band = chip // 4
    mate = me + 1 - 2 * core
    nxt = lax.rem(me + 1, CTX)
    prv = lax.rem(me + CTX - 1, CTX)

    def send(src, dst, ssem, rsem, ctx):
        return pltpu.make_async_remote_copy(
            src_ref=src, dst_ref=dst, send_sem=ssem, recv_sem=rsem,
            device_id={"ctx": ctx}, device_id_type=MESH,
        )

    barrier = pltpu.get_barrier_semaphore()

    def greet_ctx(i):
        pl.semaphore_signal(
            barrier, inc=1, device_id={"ctx": lax.rem(me + i, CTX)}, device_id_type=MESH
        )

    def greet_dp(i):
        pl.semaphore_signal(
            barrier, inc=1, device_id={"dp": lax.rem(zed + i, DPS)}, device_id_type=MESH
        )

    loop(1, CTX, greet_ctx)
    loop(1, DPS, greet_dp)

    rows = lax.broadcasted_iota(jnp.int32, (TOK, 128), 0)
    lanes = lax.broadcasted_iota(jnp.int32, (TOK, 128), 1)
    lower = rows >= lanes
    left = lanes < WIDTH

    ldp[...] = jnp.zeros((TOK, 128), F32)
    ldp[:, :HEADS] = ld_ref[...] * LOG2E
    sums = dot(lower.astype(F32), ldp[...], precision=lax.Precision.HIGHEST)
    dst[...] = sums.T
    decay = jnp.exp2(sums[TOK - 1 : TOK, :])
    dec[...] = jnp.broadcast_to(decay, (8, 128))
    xe[0:8, :] = jnp.zeros((8, CH), F32)

    pl.semaphore_wait(barrier, CTX - 1 + DPS - 1)

    halo_copy = send(x_ref.at[pl.ds(TOK - 16, 16), :], halo, h_sem.at[0], h_sem.at[1], nxt)
    halo_copy.start()
    decay_copy = send(dec, decp, d_sem.at[0], d_sem.at[1], mate)
    decay_copy.start()

    raw = raw_ref[...]
    steps = jnp.maximum(raw, 0.0) + jnp.log1p(jnp.exp(-jnp.abs(raw)))

    for h in range(HEADS):
        dsx[:, 128 * h : 128 * h + 128] = jnp.broadcast_to(sums[:, h : h + 1], (TOK, 128))
    for g in range(BLOCKS):
        c = slice(128 * g, 128 * g + 128)
        stx[:, c] = jnp.where(
            left,
            jnp.broadcast_to(steps[:, 2 * g : 2 * g + 1], (TOK, 128)),
            jnp.broadcast_to(steps[:, 2 * g + 1 : 2 * g + 2], (TOK, 128)),
        )
        onehot[c, :] = (lanes == 2 * g + (rows >= WIDTH).astype(jnp.int32)).astype(BF16)

    def expand(row, count):
        at = lax.broadcasted_iota(jnp.int32, (count, 128), 1) < WIDTH
        return [
            jnp.where(
                at,
                jnp.broadcast_to(row[:, 2 * g : 2 * g + 1], (count, 128)),
                jnp.broadcast_to(row[:, 2 * g + 1 : 2 * g + 2], (count, 128)),
            )
            for g in range(BLOCKS)
        ]

    for g, v in enumerate(expand(skip_ref[...], 1)):
        skx[:, 128 * g : 128 * g + 128] = v

    decay_copy.wait()
    mine, other = dec[0:1, :], decp[0:1, :]
    decg[chip] = dec[...] * decp[...]
    first = core == 0
    for g, (a, b) in enumerate(zip(expand(mine, 1), expand(other, 1))):
        c = slice(128 * g, 128 * g + 128)
        one = jnp.ones_like(a)
        coef[0:1, c] = jnp.where(first, b, one)
        coef[1:2, c] = jnp.where(first, one, a)
        coef[2:3, c] = jnp.where(first, one, b)
        coef[3:4, c] = jnp.where(first, a, one)
        coef[4:5, c] = a
        coef[5:6, c] = b

    def chip_at(i):
        return lax.rem(chip + i, CHIPS)

    def decay_out(q):
        return send(decg.at[chip], decg.at[chip], dg_s.at[q], dg_r.at[chip], 2 * q + core)

    def decay_in(q):
        return send(decg.at[q], decg.at[q], dg_s.at[q], dg_r.at[q], 2 * q + core)

    loop(1, CHIPS, lambda i: decay_out(chip_at(i)).start())

    xe[8:, :] = x_ref[...].astype(F32)
    halo_copy.wait()
    xe[0:8, :] = jnp.where(me > 0, halo[...].astype(F32)[8:16, :], 0.0)

    def conv(j):
        c = cols(j)
        pre = jnp.broadcast_to(b_ref[:, c], (TOK, 128))
        for k in range(TAPS):
            pre = pre + w_ref[k : k + 1, c] * xe[5 + k : 5 + k + TOK, c]
        sig = 1.0 / (1.0 + jnp.exp(-pre))
        act[:, c] = (pre * sig).astype(BF16)
        dsil[:, c] = sig * (1.0 + pre * (1.0 - sig))

    loop(0, CH // 128, conv)

    inject = act[:, SIG : SIG + STATE]
    readout = act[:, SIG + STATE :]
    inject_t = inject.T
    readout_t = readout.T

    def scaled(g):
        c = cols(g)
        ds = jnp.where(left, dsx[:, cols(2 * g)], dsx[:, cols(2 * g + 1)])
        start = jnp.exp2(ds)
        end = jnp.exp2(ds[TOK - 1 : TOK, :] - ds)
        fsx[:, c] = start
        tex[:, c] = end
        s = act[:, c].astype(F32)
        t = cot_ref[:, c].astype(F32)
        step = stx[:, c]
        tail[:, c] = (s * (step * end)).astype(BF16)
        sst[:, c] = (s * step).astype(BF16)
        gst[:, c] = (t * start).astype(BF16)
        skp[:, c] = jnp.sum((s * t).reshape(TOK // 8, 8, 128), axis=0)

    def pair_one(j):
        c = cols(j, GW)
        there = pl.ds(pl.multiple_of(HALF * (1 - core), HALF), HALF)
        return send(loc.at[:, there, c], prt.at[:, :, c], p1_s.at[j], p1_r.at[j], mate)

    def local_group(j):
        loop(0, GB, lambda i: scaled(j * GB + i))
        c = cols(j, GW)
        loc[0, :, c] = dot(inject_t, tail[:, c]).astype(BF16)
        loc[1, :, c] = dot(readout_t, gst[:, c]).astype(BF16)
        pair_one(j).start()

    loop(0, GROUPS, local_group)

    here = pl.ds(pl.multiple_of(HALF * core, HALF), HALF)

    def piece(ref, q):
        r = pl.ds(pl.multiple_of(ROWS * (q // 4), ROWS), ROWS)
        return ref.at[:, r, cols(lax.rem(q, 4), GW)]

    def state_out(q):
        return send(piece(tsum, q), rcv.at[chip], a_s.at[q], a_r.at[chip], 2 * q + core)

    def state_in(q):
        return send(piece(tsum, q), rcv.at[q], a_s.at[q], a_r.at[q], 2 * q + core)

    def chip_group(j):
        pair_one(j).wait_recv()
        c = cols(j, GW)
        tsum[0, :, c] = (
            coef[0:1, c] * loc[0, here, c].astype(F32) + coef[1:2, c] * prt[0, :, c].astype(F32)
        ).astype(BF16)
        tsum[1, :, c] = (
            coef[2:3, c] * loc[1, here, c].astype(F32) + coef[3:4, c] * prt[1, :, c].astype(F32)
        ).astype(BF16)

        def out(r):
            q = 4 * r + j

            @pl.when(q != chip)
            def _():
                state_out(q).start()

        loop(0, 4, out)

    loop(0, GROUPS, chip_group)
    own_piece = pl.ds(pl.multiple_of(ROWS * band, ROWS), ROWS)
    rcv[chip] = tsum[:, own_piece, cols(quarter, GW)]

    scores = dot(readout, inject, ((1,), (1,)))
    scores_t = dot(inject, readout, ((1,), (1,)))
    low_scores = jnp.where(lower, scores, 0.0)
    up_scores = jnp.where(rows <= lanes, scores_t, 0.0)
    run[...] = jnp.zeros((TOK, 128), F32)
    lane_a = left.astype(BF16)
    lane_b = (lanes >= WIDTH).astype(BF16)

    def intra(g):
        c = cols(g)
        fades = []
        for e in range(2):
            gap = dsx[:, cols(2 * g + e)] - dst[pl.ds(2 * g + e, 1), :]
            fades.append(jnp.exp2(jnp.where(lower, gap, -gap)))
        mix = jnp.concatenate([(f * low_scores).astype(BF16) for f in fades], axis=1)
        mix_t = jnp.concatenate([(f * up_scores).astype(BF16) for f in fades], axis=1)
        s = sst[:, c]
        t = cot_ref[:, c]
        both = jnp.concatenate([s * lane_a, s * lane_b], axis=0)
        oi[:, c] = dot(mix, both)
        bi[:, c] = dot(mix_t, jnp.concatenate([t * lane_a, t * lane_b], axis=0))
        inner = dot(t, both, ((1,), (1,)))
        run[...] += fades[0] * inner[:, :128] + fades[1] * inner[:, 128:]

    loop(0, SPLIT, intra)

    def decays_in(i):
        decay_in(chip_at(i)).wait_recv()

    loop(1, CHIPS, decays_in)
    all_decays = decg[:, 0, :]
    for g, v in enumerate(expand(all_decays, CHIPS)):
        dcx[:, 128 * g : 128 * g + 128] = v
    loop(1, CHIPS, lambda i: state_in(chip_at(i)).wait_recv())
    qc = cols(quarter, GW)

    def forward(q, carry):
        res[q, 0] = carry.astype(BF16)
        return dcx[pl.ds(q, 1), qc] * carry + rcv[q, 0].astype(F32)

    def backward(i, carry):
        q = CHIPS - 1 - i
        res[q, 1] = carry.astype(BF16)
        return dcx[pl.ds(q, 1), qc] * carry + rcv[q, 1].astype(F32)

    zero = jnp.zeros((ROWS, GW), F32)
    lax.fori_loop(0, CHIPS, forward, zero)
    lax.fori_loop(0, CHIPS, backward, zero)

    def result_out(q):
        return send(res.at[q], piece(inc, chip), b_s.at[q], b_r.at[chip], 2 * q + core)

    def result_in(q):
        return send(res.at[q], piece(inc, q), b_s.at[q], b_r.at[q], 2 * q + core)

    loop(1, CHIPS, lambda i: result_out(chip_at(i)).start())
    inc[:, own_piece, qc] = res[chip]

    loop(SPLIT, BLOCKS, intra)

    skip_rows = skp[...]
    skip_heads = sum(dot(v, onehot[...]) for v in split3(skip_rows))
    mix_total = jnp.where(lower, run[...], 0.0).astype(BF16)
    grad_readout = dot(mix_total, inject)
    grad_inject = dot(mix_total.T, readout)

    def pair_two(j):
        c = cols(j, GW)
        return send(snd.at[:, :, c], fin.at[:, here, c], p2_s.at[j], p2_r.at[j], mate)

    def spread_group(j):
        def arrive(r):
            q = 4 * r + j

            @pl.when(q != chip)
            def _():
                result_in(q).wait_recv()

        loop(0, 4, arrive)
        c = cols(j, GW)
        a, b = coef[4:5, c], coef[5:6, c]
        snd[core, :, c] = (
            a * inc[core, :, c].astype(F32) + loc[core, here, c].astype(F32)
        ).astype(BF16)
        snd[1 - core, :, c] = inc[1 - core, :, c]
        pair_two(j).start()
        fin[1 - core, here, c] = (
            b * inc[1 - core, :, c].astype(F32) + prt[1 - core, :, c].astype(F32)
        ).astype(BF16)
        fin[core, here, c] = inc[core, :, c]

    loop(0, GROUPS, spread_group)

    def finish_rows(c, grad_act):
        grad = grad_act * dsil[:, c]
        gp[0:TOK, c] = grad
        for k in range(TAPS):
            part[k : k + 1, c] = jnp.sum(grad * xe[5 + k : 5 + k + TOK, c], axis=0, keepdims=True)
        part[4:5, c] = jnp.sum(grad, axis=0, keepdims=True)

    def finish(g):
        c = cols(g)
        s = act[:, c].astype(F32)
        t = cot_ref[:, c].astype(F32)
        gain = skx[:, c]
        out = oi[:, c] + fsx[:, c] * dot(readout, fin[0, :, c]) + gain * s
        out_ref[:, c] = out.astype(BF16)
        back = bi[:, c] + tex[:, c] * dot(inject, fin[1, :, c])
        z = s * back
        z_hi = z.astype(BF16)
        zhi[:, c] = z_hi
        zlo[:, c] = (z - z_hi.astype(F32)).astype(BF16)
        finish_rows(c, stx[:, c] * back + gain * t)

    part[...] = jnp.zeros((8, CH), F32)
    part[5:6, 0:128] = jnp.sum(skip_heads, axis=0, keepdims=True)

    def finish_group(j):
        pair_two(j).wait_recv()
        loop(0, GB, lambda i: finish(j * GB + i))

    loop(0, GROUPS, finish_group)
    finish_rows(slice(SIG, SIG + STATE), grad_inject + dot(tail[...], fin[1], ((1,), (1,))))
    finish_rows(slice(SIG + STATE, CH), grad_readout + dot(gst[...], fin[0], ((1,), (1,))))

    def tile_out(j):
        return send(part.at[:, cols(j)], ar1.at[me], r1_s.at[j], r1_r.at[me], j)

    def tile_in(i):
        return send(part.at[:, cols(0)], ar1.at[i], r1_s.at[0], r1_r.at[i], i)

    def each_other(i, fn):
        @pl.when(i != me)
        def _():
            fn(i)

    loop(0, OWNERS, lambda j: each_other(j, lambda j: tile_out(j).start()))
    grad_halo = send(gp.at[pl.ds(0, 8), :], gp.at[pl.ds(TOK, 8), :], g_sem.at[0], g_sem.at[1], prv)
    grad_halo.start()

    steps_z = dot(zhi[...], onehot[...]) + dot(zlo[...], onehot[...])
    e = jnp.exp(-jnp.abs(raw))
    gate = jnp.where(raw >= 0, 1.0, e) / (1.0 + e)
    sg_ref[...] = steps_z[:, :HEADS] * gate

    def dp_out(i):
        z = lax.rem(zed + i, DPS)
        return pltpu.make_async_remote_copy(
            src_ref=sum1, dst_ref=ar2.at[zed], send_sem=r2_s.at[z], recv_sem=r2_r.at[zed],
            device_id={"dp": z}, device_id_type=MESH,
        )

    def dp_in(i):
        z = lax.rem(zed + i, DPS)
        return pltpu.make_async_remote_copy(
            src_ref=sum1, dst_ref=ar2.at[z], send_sem=r2_s.at[z], recv_sem=r2_r.at[z],
            device_id={"dp": z}, device_id_type=MESH,
        )

    def total_out(i):
        return send(tot.at[:, cols(me)], tot.at[:, cols(me)], r3_s.at[i], r3_r.at[me], i)

    def total_in(i):
        return send(tot.at[:, cols(i)], tot.at[:, cols(i)], r3_s.at[i], r3_r.at[i], i)

    owner = me < OWNERS

    @pl.when(owner)
    def _():
        loop(0, CTX, lambda i: each_other(i, lambda i: tile_in(i).wait_recv()))
        ar1[me] = part[:, cols(me)]
        sum1[...] = jnp.sum(ar1[...], axis=0)
        loop(1, DPS, lambda i: dp_out(i).start())

    grad_halo.wait_recv()
    gp[TOK:, :] = jnp.where(me < CTX - 1, gp[TOK:, :], 0.0)

    def input_grad(j):
        c = cols(j)
        total = w_ref[0:1, c] * gp[3 : 3 + TOK, c]
        for k in range(1, TAPS):
            total = total + w_ref[k : k + 1, c] * gp[3 - k : 3 - k + TOK, c]
        gin_ref[:, c] = total.astype(BF16)

    def reduce_dp():
        loop(1, DPS, lambda i: dp_in(i).wait_recv())
        ar2[zed] = sum1[...]
        tot[:, cols(me)] = jnp.sum(ar2[...], axis=0)
        loop(0, CTX, lambda i: each_other(i, lambda i: total_out(i).start()))

    pl.when(owner)(reduce_dp)

    loop(0, CH // 128, input_grad)

    loop(0, OWNERS, lambda i: each_other(i, lambda i: total_in(i).wait_recv()))
    wg_ref[...] = tot[0:TAPS, :]
    bg_ref[...] = tot[4:5, :]
    kg_ref[...] = tot[5:6, 0:HEADS]

    grad_halo.wait_send()
    loop(0, GROUPS, lambda j: (pair_one(j).wait_send(), pair_two(j).wait_send()) and None)

    def chips_done(i):
        q = chip_at(i)
        decay_out(q).wait_send()
        state_out(q).wait_send()
        result_out(q).wait_send()

    loop(1, CHIPS, chips_done)
    loop(0, OWNERS, lambda j: each_other(j, lambda j: tile_out(j).wait_send()))

    @pl.when(owner)
    def _():
        loop(1, DPS, lambda i: dp_out(i).wait_send())
        loop(0, CTX, lambda i: each_other(i, lambda i: total_out(i).wait_send()))


def scratch():
    v = pltpu.VMEM
    dma = pltpu.SemaphoreType.DMA
    return [
        v((TOK + 8, CH), F32),
        v((16, CH), BF16),
        v((TOK, CH), BF16),
        v((TOK, CH), F32),
        v((TOK, 128), F32),
        v((128, TOK), F32),
        v((TOK, HEADS * 128), F32),
        v((TOK, SIG), F32),
        v((TOK, SIG), F32),
        v((TOK, SIG), F32),
        v((TOK, SIG), BF16),
        v((TOK, SIG), BF16),
        v((TOK, SIG), BF16),
        v((2, STATE, SIG), BF16),
        v((2, HALF, SIG), BF16),
        v((8, 128), F32),
        v((8, 128), F32),
        v((CHIPS, 8, 128), F32),
        v((CHIPS, SIG), F32),
        v((8, SIG), F32),
        v((1, SIG), F32),
        v((2, HALF, SIG), BF16),
        v((CHIPS, 2, ROWS, GW), BF16),
        v((CHIPS, 2, ROWS, GW), BF16),
        v((2, HALF, SIG), BF16),
        v((2, HALF, SIG), BF16),
        v((2, STATE, SIG), BF16),
        v((TOK, SIG), F32),
        v((TOK, SIG), F32),
        v((TOK, 128), F32),
        v((TOK + 8, CH), F32),
        v((TOK, SIG), BF16),
        v((TOK, SIG), BF16),
        v((SIG, 128), BF16),
        v((8, SIG), F32),
        v((8, CH), F32),
        v((CTX, 8, 128), F32),
        v((DPS, 8, 128), F32),
        v((8, 128), F32),
        v((8, CH), F32),
        dma((2,)),
        dma((2,)),
        dma((CHIPS,)),
        dma((CHIPS,)),
        dma((GROUPS,)),
        dma((GROUPS,)),
        dma((CHIPS,)),
        dma((CHIPS,)),
        dma((CHIPS,)),
        dma((CHIPS,)),
        dma((GROUPS,)),
        dma((GROUPS,)),
        dma((2,)),
        dma((OWNERS,)),
        dma((CTX,)),
        dma((DPS,)),
        dma((DPS,)),
        dma((CTX,)),
        dma((CTX,)),
    ]


def body(conv_input, step_raw, log_decay, cotangent, conv_weight, conv_bias, skip_gain):
    vmem = pl.BlockSpec(memory_space=pltpu.VMEM)
    shapes = (
        jax.ShapeDtypeStruct((TOK, SIG), BF16),
        jax.ShapeDtypeStruct((TOK, CH), BF16),
        jax.ShapeDtypeStruct((TOK, HEADS), F32),
        jax.ShapeDtypeStruct((TAPS, CH), F32),
        jax.ShapeDtypeStruct((1, CH), F32),
        jax.ShapeDtypeStruct((1, HEADS), F32),
    )
    out, gin, sg, wg, bg, kg = pl.pallas_call(
        kernel,
        out_shape=shapes,
        in_specs=[vmem] * 7,
        out_specs=[vmem] * 6,
        scratch_shapes=scratch(),
        compiler_params=pltpu.CompilerParams(
            collective_id=0, has_side_effects=True, vmem_limit_bytes=52 * 1024 * 1024
        ),
    )(
        conv_input[0], step_raw[0], log_decay[0], cotangent[0],
        conv_weight, conv_bias[None], skip_gain[None],
    )
    return out[None], gin[None], sg[None], wg, bg[0], kg[0]


def solution(mesh):
    split = P("dp", "ctx", None)
    return jax.shard_map(
        body,
        mesh=mesh,
        in_specs=(split, split, split, split, P(), P(), P()),
        out_specs=(split, split, split, P(), P(), P()),
        check_vma=False,
    )
```

time: 485 us -> 72.3 us (0.15)
  waiting for transfers between devices: 245 us -> 0 us
  blocking collectives: 98.4 us -> 0 us
  Pallas kernels: 0 us -> 63.9 us
  other arithmetic: 60.2 us -> 0.63 us
  local copies, waits for them, and re-layouts: 32.4 us -> 6.79 us
  matrix products: 21.2 us -> 0 us
  between operations: 14.4 us -> 0.69 us
  starting transfers between devices: 9.12 us -> 0 us
    all_gather x2 -> x0, waiting for transfers between devices: 245 us -> none  [entering(): gathered = jax.tree.map(lambda a: lax.all_gather(a, axis), part)]
    psum x1 -> x0, blocking collectives: 74.9 us -> none  [body(): lax.psum((weight_part, bias_part, skip_part), ('dp', 'ctx'))]
    pallas_call x0 -> x1, Pallas kernels: none -> 63.9 us  [body(): pl.pallas_call(kernel, out_shape=shapes, in_specs=[vmem] * 7, out_specs=[...]
    add x31 -> x0, other arithmetic: 48.8 us -> none  [join_pairs(): latter[0][:, None, None] * earlier[1] + latter[1]]
    all_gather x1 -> x0, blocking collectives: 23.5 us -> none  [entering(): gathered = jax.tree.map(lambda a: lax.all_gather(a, axis), part)]
    mul x31 -> x0, local copies, waits for them, and re-layouts: 21.3 us -> none  [join_pairs(): latter[0][:, None, None] * earlier[1] + latter[1]]
    dot_general x13 -> x0, matrix products: 21.2 us -> none  [the longest x1 3.53 us: body(): jnp.einsum('thp,shp->hts', grad_group, signal_group, preferred_element_ty...]
    ppermute x2 -> x0, starting transfers between devices: 9.04 us -> none  [passed_along(): lax.ppermute(value, axis, [(source, source + steps) for source in range(l...]
  transfers between devices with their start and end apart: 4 -> 0, of which waited for: 2 -> 0; matrix products, arithmetic and copies ran while one was open for 5% -> 0% of each run, Pallas kernels for 0% -> 0%
where the time goes in v1:
time: 72.3 us; the launch traced here: 72 us
  Pallas kernels  63.9 us (88%)
  local copies, waits for them, and re-layouts  6.79 us (9%)
    pallas_call x1, Pallas kernels, body(): pl.pallas_call(kernel, out_shape=shapes, in_specs=[vmem] * 7, out_specs=[...  63.9 us
    unnamed x19, local copies, waits for them, and re-layouts  6.07 us

profile of v1, /device:TPU:1, one launch (start us, length us, event | category | flops | bytes accessed | tf_op | source)
XLA Modules:
  0.0 72.0 jit_solution(10071158009557958792)
XLA Ops:
  0.6 0.0 copy-start.4
  0.6 0.7 %broadcast_in_dim.15.b_ref = f32[1,2816]{1,0:T(1,128)S(1)} reshape(f32[2816]{0:T(1024)} %param.12) | data formatting | bytes 22528 | tf_op jit(solution)/shard_map/broadcast_in_dim | solution.py:557
  1.4 0.0 copy-done.4
  1.4 0.0 copy-start.5
  1.4 0.1 copy.13
  1.5 0.0 copy-start.1
  1.5 0.6 copy-done.5
  2.1 0.1 copy.14
  2.2 0.0 copy-start.2
  2.2 0.1 copy-done.1
  2.3 0.6 copy-done.2
  2.9 0.0 copy-start
  2.9 1.1 %copy-done = bf16[1,128,2560]{2,1,0:T(8,128)(2,1)S(1)} copy-done((bf16[1,128,2560]{2,1,0:T(8,128)(2,1)S(1)}, bf16[1,128,2560]{2,1,0:T(8,128)(2,1)}, u32[]{:S(2)}) %copy-start) | copy-done | bytes 655384
  4.0 63.9 %shard_map.118 = (bf16[128,2560]{1,0:T(8,128)(2,1)S(1)}, bf16[128,2816]{1,0:T(8,128)(2,1)}, f32[128,40]{1,0:T(8,128)S(1)}, f32[4,2816]{1,0:T(4,128)S(1)}, f32[1,2816]{1,0:T(1,128)S(1)}, /*index=5*/f32[1,40]{1,0:T(1,128)S(1)}) custom-call(bf16[128,2816]{1,0:T(8,128)(2,1)} %bitcast.16, f32[128,40]{1,0:T(8,128)S(1)} %bitcast.11, f32[128,40]{1,0:T(8,128)S(1)} %bitcast.12, ...), custom_call_target="tpu_custom_call" | custom-call | tf_op jit(solution)/shard_map/pallas_call | solution.py:546
  67.9 0.0 copy-start.3
  67.9 0.6 reduce
  68.5 0.7 copy.15
  69.2 0.8 %copy.20 = bf16[1,128,2560]{2,1,0:T(8,128)(2,1)} copy(bf16[1,128,2560]{2,1,0:T(8,128)(2,1)S(1)} %bitcast.10) | data formatting | bytes 1310720
  70.0 0.0 copy-done.3
  70.1 0.9 %copy.21 = bf16[1,128,2816]{2,1,0:T(8,128)(2,1)} copy(bf16[1,128,2816]{2,1,0:T(8,128)(2,1)S(1)} %bitcast.17) | data formatting | bytes 1441792
  70.9 0.6 copy.22
  71.5 0.5 copy.23
Async XLA Ops:
  0.6 0.7 %copy-start.4 = (f32[1,128,40]{1,2,0:T(8,128)S(1)}, f32[1,128,40]{1,2,0:T(8,128)}, u32[]{:S(2)}) copy-start(f32[1,128,40]{1,2,0:T(8,128)} %param.8) | copy-start | bytes 61444
  1.4 0.7 %copy-start.5 = (f32[1,128,40]{1,2,0:T(8,128)S(1)}, f32[1,128,40]{1,2,0:T(8,128)}, u32[]{:S(2)}) copy-start(f32[1,128,40]{1,2,0:T(8,128)} %param.9) | copy-start | bytes 61444
  1.5 0.8 %copy-start.1 = (f32[4,2816]{1,0:T(4,128)S(1)}, f32[4,2816]{1,0:T(4,128)}, u32[]{:S(2)}) copy-start(f32[4,2816]{1,0:T(4,128)} %w_ref.1) | copy-start | bytes 135172
  2.2 0.7 copy-start.2
  2.9 1.1 %copy-start = (bf16[1,128,2560]{2,1,0:T(8,128)(2,1)S(1)}, bf16[1,128,2560]{2,1,0:T(8,128)(2,1)}, u32[]{:S(2)}) copy-start(bf16[1,128,2560]{2,1,0:T(8,128)(2,1)} %param.10) | copy-start | bytes 1966084
  67.9 2.2 %copy-start.3 = (bf16[128,2816]{1,0:T(8,128)(2,1)S(1)}, bf16[128,2816]{1,0:T(8,128)(2,1)}, u32[]{:S(2)}) copy-start(bf16[128,2816]{1,0:T(8,128)(2,1)} %get-tuple-element.13) | copy-start | bytes 2162692

commit v2 on v1

v2 whole, which is shorter than its diff:
```python
import jax
import jax.numpy as jnp
from jax import lax
from jax.experimental import pallas as pl
from jax.experimental.pallas import tpu as pltpu
from jax.sharding import PartitionSpec as P

HEADS = 40
WIDTH = 64
STATE = 128
TAPS = 4
TOK = 128
SIG = HEADS * WIDTH
CH = SIG + 2 * STATE
BLOCKS = SIG // 128
CTX = 32
CHIPS = 16
DPS = 8
GROUPS = 4
GW = SIG // GROUPS
GB = GW // 128
HALF = STATE // 2
ROWS = 16
OWNERS = CH // 128
SPLIT_A = 6
SPLIT_B = 13
VMEM = 60 * 1024 * 1024
LOG2E = 1.4426950408889634
F32 = jnp.float32
BF16 = jnp.bfloat16
MESH = pl.DeviceIdType.MESH


def dot(a, b, dims=((1,), (0,)), **kw):
    return lax.dot_general(a, b, (dims, ((), ())), preferred_element_type=F32, **kw)


def split3(v):
    hi = v.astype(BF16)
    rest = v - hi.astype(F32)
    mid = rest.astype(BF16)
    low = (rest - mid.astype(F32)).astype(BF16)
    return hi, mid, low


def loop(lo, hi, fn):
    def step(i, carry):
        fn(i)
        return carry

    lax.fori_loop(lo, hi, step, 0)


def cols(i, width=128):
    return pl.ds(pl.multiple_of(i * width, 128), width)


def kernel(
    x_hbm, raw_hbm, ld_hbm, cot_hbm, w_hbm, b_hbm, skip_hbm,
    out_hbm, gin_hbm, sg_ref, wg_ref, bg_ref, kg_ref,
    out_ref, gin_ref, xb, cot_ref, w_ref, b_ref, skip_ref, raw_ref,
    xe, halo, act, dsil, ldp, stp, dst, dsx, stx, fsx, tex, tail, gst, sst,
    loc, prt, dec, decp, decg, dcx, coef, skx, tsum, rcv, res, inc, snd, fin,
    oi, bi, run, gp, zhi, zlo, onehot, skp, part, ar1, ar2, sum1, tot,
    in_sem, o_sem, h_sem, d_sem, dg_s, dg_r, p1_s, p1_r, a_s, a_r, b_s, b_r, p2_s, p2_r, g_sem,
    r1_s, r1_r, r2_s, r2_r, r3_s, r3_r,
):
    me = lax.axis_index("ctx")
    zed = lax.axis_index("dp")
    core = lax.rem(me, 2)
    chip = me // 2
    quarter = lax.rem(chip, 4)
    band = chip // 4
    mate = me + 1 - 2 * core
    nxt = lax.rem(me + 1, CTX)
    prv = lax.rem(me + CTX - 1, CTX)
    first = core == 0

    def send(src, dst, ssem, rsem, ctx):
        return pltpu.make_async_remote_copy(
            src_ref=src, dst_ref=dst, send_sem=ssem, recv_sem=rsem,
            device_id={"ctx": ctx}, device_id_type=MESH,
        )

    barrier = pltpu.get_barrier_semaphore()

    def greet_ctx(i):
        pl.semaphore_signal(
            barrier, inc=1, device_id={"ctx": lax.rem(me + i, CTX)}, device_id_type=MESH
        )

    def greet_dp(i):
        pl.semaphore_signal(
            barrier, inc=1, device_id={"dp": lax.rem(zed + i, DPS)}, device_id_type=MESH
        )

    fetch = [
        pltpu.make_async_copy(src, dst, in_sem.at[i])
        for i, (src, dst) in enumerate((
            (ld_hbm, ldp.at[pl.ds(0, HEADS), :]), (raw_hbm, raw_ref), (x_hbm, xb), (cot_hbm, cot_ref),
            (w_hbm, w_ref), (b_hbm, b_ref), (skip_hbm, skip_ref),
        ))
    ]
    for copy in fetch:
        copy.start()
    loop(1, CTX, greet_ctx)
    loop(1, DPS, greet_dp)

    rows = lax.broadcasted_iota(jnp.int32, (TOK, 128), 0)
    lanes = lax.broadcasted_iota(jnp.int32, (TOK, 128), 1)
    lower = rows >= lanes
    left = lanes < WIDTH

    ldp[HEADS:, :] = jnp.zeros((128 - HEADS, TOK), F32)
    stp[...] = jnp.zeros((128, TOK), F32)
    xe[0:8, :] = jnp.zeros((8, CH), F32)
    for copy in fetch:
        copy.wait()

    sums_t = dot(ldp[...] * LOG2E, (rows <= lanes).astype(F32), precision=lax.Precision.HIGHEST)
    dst[...] = sums_t
    sums = sums_t.T
    decay = jnp.exp2(sums[TOK - 1 : TOK, :])
    dec[...] = jnp.broadcast_to(decay, (8, 128))
    raw = raw_ref[...]
    stp[0:HEADS, :] = jnp.maximum(raw, 0.0) + jnp.log1p(jnp.exp(-jnp.abs(raw)))
    steps = stp[...].T

    for h in range(HEADS):
        dsx[:, 128 * h : 128 * h + 128] = jnp.broadcast_to(sums[:, h : h + 1], (TOK, 128))
    for g in range(BLOCKS):
        c = slice(128 * g, 128 * g + 128)
        stx[:, c] = jnp.where(
            left,
            jnp.broadcast_to(steps[:, 2 * g : 2 * g + 1], (TOK, 128)),
            jnp.broadcast_to(steps[:, 2 * g + 1 : 2 * g + 2], (TOK, 128)),
        )
        onehot[c, :] = (lanes == 2 * g + (rows >= WIDTH).astype(jnp.int32)).astype(BF16)

    def expand(row, count):
        at = lax.broadcasted_iota(jnp.int32, (count, 128), 1) < WIDTH
        return [
            jnp.where(
                at,
                jnp.broadcast_to(row[:, 2 * g : 2 * g + 1], (count, 128)),
                jnp.broadcast_to(row[:, 2 * g + 1 : 2 * g + 2], (count, 128)),
            )
            for g in range(BLOCKS)
        ]

    for g, v in enumerate(expand(skip_ref[...], 1)):
        skx[:, 128 * g : 128 * g + 128] = v

    def conv(j, r0, n):
        c = cols(j)
        pre = jnp.broadcast_to(b_ref[pl.ds(j, 1), :], (n, 128))
        for k in range(TAPS):
            pre = pre + w_ref[k : k + 1, c] * xe[5 + k + r0 : 5 + k + r0 + n, c]
        sig = 1.0 / (1.0 + jnp.exp(-pre))
        act[r0 : r0 + n, c] = (pre * sig).astype(BF16)
        dsil[r0 : r0 + n, c] = sig * (1.0 + pre * (1.0 - sig))

    def starts(g):
        c = cols(g)
        ds = jnp.where(left, dsx[:, cols(2 * g)], dsx[:, cols(2 * g + 1)])
        start = jnp.exp2(ds)
        fsx[:, c] = start
        tex[:, c] = jnp.exp2(ds[TOK - 1 : TOK, :] - ds)
        gst[:, c] = (cot_ref[:, c].astype(F32) * start).astype(BF16)

    def scaled(g, r0, n):
        c = cols(g)
        r = slice(r0, r0 + n)
        s = act[r, c].astype(F32)
        step = stx[r, c]
        tail[r, c] = (s * (step * tex[r, c])).astype(BF16)
        sst[r, c] = (s * step).astype(BF16)

    def later_rows(j):
        c = cols(j)
        xe[8:, c] = xb[:, c].astype(F32)
        conv(j, ROWS, TOK - ROWS)

    def later_signal(g):
        later_rows(g)
        starts(g)
        scaled(g, ROWS, TOK - ROWS)

    loop(0, BLOCKS, later_signal)
    loop(BLOCKS, BLOCKS + 2, later_rows)

    pl.semaphore_wait(barrier, CTX - 1 + DPS - 1)

    halo_copy = send(xb.at[pl.ds(TOK - 16, 16), :], halo, h_sem.at[0], h_sem.at[1], nxt)
    halo_copy.start()
    decay_copy = send(dec, decp, d_sem.at[0], d_sem.at[1], mate)
    decay_copy.start()

    decay_copy.wait()
    mine, other = dec[0:1, :], decp[0:1, :]
    decg[chip] = dec[...] * decp[...]

    def chip_at(i):
        return lax.rem(chip + i, CHIPS)

    def decay_out(q):
        return send(decg.at[chip], decg.at[chip], dg_s.at[q], dg_r.at[chip], 2 * q + core)

    def decay_in(q):
        return send(decg.at[q], decg.at[q], dg_s.at[q], dg_r.at[q], 2 * q + core)

    loop(1, CHIPS, lambda i: decay_out(chip_at(i)).start())
    for g, (a, b) in enumerate(zip(expand(mine, 1), expand(other, 1))):
        c = slice(128 * g, 128 * g + 128)
        coef[0:1, c] = a
        coef[1:2, c] = b

    halo_copy.wait_recv()
    xe[0:8, :] = jnp.where(me > 0, halo[...].astype(F32)[8:16, :], 0.0)
    loop(BLOCKS, BLOCKS + 2, lambda j: conv(j, 0, ROWS))
    inject = act[:, SIG : SIG + STATE]
    readout = act[:, SIG + STATE :]

    def pair_one(k, j):
        c = cols(j, GW)
        there = pl.ds(pl.multiple_of(HALF * (1 - core), HALF), HALF)
        return send(loc.at[k, there, c], prt.at[k, :, c], p1_s.at[k, j], p1_r.at[k, j], mate)

    readout_t = readout.T

    def local_adjoint(j):
        c = cols(j, GW)
        loc[1, :, c] = dot(readout_t, gst[:, c]).astype(BF16)
        pair_one(1, j).start()

    loop(0, GROUPS, local_adjoint)

    def early_rows(g):
        conv(g, 0, ROWS)
        scaled(g, 0, ROWS)

    loop(0, BLOCKS, early_rows)
    inject_t = inject.T

    def local_state(j):
        c = cols(j, GW)
        loc[0, :, c] = dot(inject_t, tail[:, c]).astype(BF16)
        pair_one(0, j).start()

    here = pl.ds(pl.multiple_of(HALF * core, HALF), HALF)
    own_rows = pl.ds(pl.multiple_of(ROWS * band, ROWS), ROWS)
    qc = cols(quarter, GW)

    def piece(ref, k, q):
        r = pl.ds(pl.multiple_of(ROWS * (q // 4), ROWS), ROWS)
        return ref.at[k, r, cols(lax.rem(q, 4), GW)]

    def state_out(k, q):
        return send(
            piece(tsum, k, q), rcv.at[k, chip], a_s.at[k, q], a_r.at[k, chip], 2 * q + core
        )

    def state_in(k, q):
        return send(piece(tsum, k, q), rcv.at[k, q], a_s.at[k, q], a_r.at[k, q], 2 * q + core)

    def chip_sums(k):
        def group(j):
            pair_one(k, j).wait_recv()
            c = cols(j, GW)
            a, b = coef[0:1, c], coef[1:2, c]
            own = loc[k, here, c].astype(F32)
            far = prt[k, :, c].astype(F32)
            if k == 0:
                total = jnp.where(first, b * own + far, a * far + own)
            else:
                total = jnp.where(first, a * far + own, b * own + far)
            tsum[k, :, c] = total.astype(BF16)

            def out(r):
                q = 4 * r + j

                @pl.when(q != chip)
                def _():
                    state_out(k, q).start()

            loop(0, 4, out)

        loop(0, GROUPS, group)
        rcv[k, chip] = tsum[k, own_rows, qc]

    chip_sums(1)
    loop(0, GROUPS, local_state)
    chip_sums(0)

    scores = dot(readout, inject, ((1,), (1,)))
    scores_t = dot(inject, readout, ((1,), (1,)))
    low_scores = jnp.where(lower, scores, 0.0)
    up_scores = jnp.where(rows <= lanes, scores_t, 0.0)
    run[...] = jnp.zeros((TOK, 128), F32)
    lane_a = left.astype(BF16)
    lane_b = (lanes >= WIDTH).astype(BF16)

    def intra(g):
        c = cols(g)
        fades = []
        for e in range(2):
            gap = dsx[:, cols(2 * g + e)] - dst[pl.ds(2 * g + e, 1), :]
            fades.append(jnp.exp2(jnp.where(lower, gap, -gap)))
        mix = jnp.concatenate([(f * low_scores).astype(BF16) for f in fades], axis=1)
        mix_t = jnp.concatenate([(f * up_scores).astype(BF16) for f in fades], axis=1)
        s = sst[:, c]
        t = cot_ref[:, c]
        both = jnp.concatenate([s * lane_a, s * lane_b], axis=0)
        oi[:, c] = dot(mix, both)
        bi[:, c] = dot(mix_t, jnp.concatenate([t * lane_a, t * lane_b], axis=0))
        inner = dot(t, both, ((1,), (1,)))
        run[...] += fades[0] * inner[:, :128] + fades[1] * inner[:, 128:]
        skp[:, c] = jnp.sum((act[:, c].astype(F32) * t.astype(F32)).reshape(TOK // 8, 8, 128), axis=0)

    loop(0, SPLIT_A, intra)

    loop(1, CHIPS, lambda i: decay_in(chip_at(i)).wait_recv())
    for g, v in enumerate(expand(decg[:, 0, :], CHIPS)):
        dcx[:, 128 * g : 128 * g + 128] = v

    def result_out(k, q):
        return send(res.at[k, q], piece(inc, k, chip), b_s.at[k, q], b_r.at[k, chip], 2 * q + core)

    def result_in(k, q):
        return send(res.at[k, q], piece(inc, k, q), b_s.at[k, q], b_r.at[k, q], 2 * q + core)

    def scan(k):
        loop(1, CHIPS, lambda i: state_in(k, chip_at(i)).wait_recv())

        def step(i, carry):
            q = i if k == 0 else CHIPS - 1 - i
            res[k, q] = carry.astype(BF16)
            return dcx[pl.ds(q, 1), qc] * carry + rcv[k, q].astype(F32)

        lax.fori_loop(0, CHIPS, step, jnp.zeros((ROWS, GW), F32))
        loop(1, CHIPS, lambda i: result_out(k, chip_at(i)).start())
        inc[k, own_rows, qc] = res[k, chip]

    scan(1)
    loop(SPLIT_A, SPLIT_B, intra)
    scan(0)
    loop(SPLIT_B, BLOCKS, intra)

    skip_heads = sum(dot(v, onehot[...]) for v in split3(skp[...]))
    mix_total = jnp.where(lower, run[...], 0.0).astype(BF16)
    grad_readout = dot(mix_total, inject)
    grad_inject = dot(mix_total.T, readout)
    part[...] = jnp.zeros((8, CH), F32)
    part[5:6, 0:128] = jnp.sum(skip_heads, axis=0, keepdims=True)

    def pair_two(k, j):
        c = cols(j, GW)
        return send(snd.at[k, :, c], fin.at[k, here, c], p2_s.at[k, j], p2_r.at[k, j], mate)

    def spread(k):
        def group(j):
            def arrive(r):
                q = 4 * r + j

                @pl.when(q != chip)
                def _():
                    result_in(k, q).wait_recv()

            loop(0, 4, arrive)
            c = cols(j, GW)
            came = inc[k, :, c]
            wide = came.astype(F32)
            near = (coef[0:1, c] * wide + loc[k, here, c].astype(F32)).astype(BF16)
            far = (coef[1:2, c] * wide + prt[k, :, c].astype(F32)).astype(BF16)
            if k == 0:
                snd[k, :, c] = jnp.where(first, near, came)
                fin[k, here, c] = jnp.where(first, came, far)
            else:
                snd[k, :, c] = jnp.where(first, came, near)
                fin[k, here, c] = jnp.where(first, far, came)
            pair_two(k, j).start()

        loop(0, GROUPS, group)

    spread(1)

    def tile_out(j):
        return send(part.at[:, cols(j)], ar1.at[me], r1_s.at[j], r1_r.at[me], j)

    def tile_in(i):
        return send(part.at[:, cols(0)], ar1.at[i], r1_s.at[0], r1_r.at[i], i)

    def each_other(i, fn):
        @pl.when(i != me)
        def _():
            fn(i)

    def finish_rows(j, grad_act):
        c = cols(j)
        grad = grad_act * dsil[:, c]
        gp[0:TOK, c] = grad
        for k in range(TAPS):
            part[k : k + 1, c] = jnp.sum(grad * xe[5 + k : 5 + k + TOK, c], axis=0, keepdims=True)
        part[4:5, c] = jnp.sum(grad, axis=0, keepdims=True)
        each_other(j, lambda j: tile_out(j).start())

    def finish(g):
        c = cols(g)
        s = act[:, c].astype(F32)
        t = cot_ref[:, c].astype(F32)
        back = bi[:, c] + tex[:, c] * dot(inject, fin[1, :, c])
        z = s * back
        z_hi = z.astype(BF16)
        zhi[:, c] = z_hi
        zlo[:, c] = (z - z_hi.astype(F32)).astype(BF16)
        finish_rows(g, stx[:, c] * back + skx[:, c] * t)

    def finish_group(j):
        pair_two(1, j).wait_recv()
        loop(0, GB, lambda i: finish(j * GB + i))

    loop(0, GROUPS, finish_group)
    finish_rows(BLOCKS, grad_inject + dot(tail[...], fin[1], ((1,), (1,))))
    spread(0)
    loop(0, GROUPS, lambda j: pair_two(0, j).wait_recv())
    finish_rows(BLOCKS + 1, grad_readout + dot(gst[...], fin[0], ((1,), (1,))))

    grad_halo = send(gp.at[pl.ds(0, 8), :], gp.at[pl.ds(TOK, 8), :], g_sem.at[0], g_sem.at[1], prv)
    grad_halo.start()

    def output(g):
        c = cols(g)
        out = oi[:, c] + fsx[:, c] * dot(readout, fin[0, :, c]) + skx[:, c] * act[:, c].astype(F32)
        out_ref[:, c] = out.astype(BF16)

    loop(0, BLOCKS, output)
    out_copy = pltpu.make_async_copy(out_ref, out_hbm, o_sem.at[0])
    out_copy.start()

    def dp_out(i):
        z = lax.rem(zed + i, DPS)
        return pltpu.make_async_remote_copy(
            src_ref=sum1, dst_ref=ar2.at[zed], send_sem=r2_s.at[z], recv_sem=r2_r.at[zed],
            device_id={"dp": z}, device_id_type=MESH,
        )

    def dp_in(i):
        z = lax.rem(zed + i, DPS)
        return pltpu.make_async_remote_copy(
            src_ref=sum1, dst_ref=ar2.at[z], send_sem=r2_s.at[z], recv_sem=r2_r.at[z],
            device_id={"dp": z}, device_id_type=MESH,
        )

    def total_out(i):
        return send(tot.at[:, cols(me)], tot.at[:, cols(me)], r3_s.at[i], r3_r.at[me], i)

    def total_in(i):
        return send(tot.at[:, cols(i)], tot.at[:, cols(i)], r3_s.at[i], r3_r.at[i], i)

    owner = me < OWNERS

    @pl.when(owner)
    def _():
        loop(0, CTX, lambda i: each_other(i, lambda i: tile_in(i).wait_recv()))
        ar1[me] = part[:, cols(me)]
        sum1[...] = jnp.sum(ar1[...], axis=0)
        loop(1, DPS, lambda i: dp_out(i).start())

    steps_z = dot(zhi[...], onehot[...]) + dot(zlo[...], onehot[...])
    e = jnp.exp(-jnp.abs(raw))
    gate = jnp.where(raw >= 0, 1.0, e) / (1.0 + e)
    sg_ref[...] = steps_z.T[0:HEADS, :] * gate

    grad_halo.wait_recv()
    gp[TOK:, :] = jnp.where(me < CTX - 1, gp[TOK:, :], 0.0)

    def input_grad(j):
        c = cols(j)
        total = w_ref[0:1, c] * gp[3 : 3 + TOK, c]
        for k in range(1, TAPS):
            total = total + w_ref[k : k + 1, c] * gp[3 - k : 3 - k + TOK, c]
        gin_ref[:, c] = total.astype(BF16)

    loop(0, CH // 256, input_grad)

    @pl.when(owner)
    def _():
        loop(1, DPS, lambda i: dp_in(i).wait_recv())
        ar2[zed] = sum1[...]
        tot[:, cols(me)] = jnp.sum(ar2[...], axis=0)
        loop(0, CTX, lambda i: each_other(i, lambda i: total_out(i).start()))

    loop(CH // 256, CH // 128, input_grad)
    gin_copy = pltpu.make_async_copy(gin_ref, gin_hbm, o_sem.at[1])
    gin_copy.start()

    halo_copy.wait_send()
    grad_halo.wait_send()

    def pairs_done(j):
        for k in range(2):
            pair_one(k, j).wait_send()
            pair_two(k, j).wait_send()

    def chips_done(i):
        q = chip_at(i)
        decay_out(q).wait_send()
        for k in range(2):
            state_out(k, q).wait_send()
            result_out(k, q).wait_send()

    loop(0, GROUPS, pairs_done)
    loop(1, CHIPS, chips_done)
    loop(0, OWNERS, lambda j: each_other(j, lambda j: tile_out(j).wait_send()))

    loop(0, OWNERS, lambda i: each_other(i, lambda i: total_in(i).wait_recv()))
    wg_ref[...] = tot[0:TAPS, :]
    for j in range(OWNERS):
        bg_ref[j : j + 1, :] = tot[4:5, 128 * j : 128 * j + 128]
    kg_ref[...] = tot[5:6, 0:HEADS]
    out_copy.wait()
    gin_copy.wait()

    @pl.when(owner)
    def _():
        loop(1, DPS, lambda i: dp_out(i).wait_send())
        loop(0, CTX, lambda i: each_other(i, lambda i: total_out(i).wait_send()))


def copy_kernel(*refs):
    n = (len(refs) - 1) // 2
    sem = refs[-1]
    copies = [
        pltpu.make_async_copy(refs[i], refs[n + i], sem.at[i]) for i in range(n)
    ]
    for copy in copies:
        copy.start()
    for copy in copies:
        copy.wait()


def scratch():
    v = pltpu.VMEM
    dma = pltpu.SemaphoreType.DMA
    return [
        v((TOK, SIG), BF16),
        v((TOK, CH), BF16),
        v((TOK, CH), BF16),
        v((TOK, SIG), BF16),
        v((TAPS, CH), F32),
        v((OWNERS, 128), F32),
        v((1, HEADS), F32),
        v((HEADS, TOK), F32),
        v((TOK + 8, CH), F32),
        v((16, CH), BF16),
        v((TOK, CH), BF16),
        v((TOK, CH), F32),
        v((128, TOK), F32),
        v((128, TOK), F32),
        v((128, TOK), F32),
        v((TOK, HEADS * 128), F32),
        v((TOK, SIG), F32),
        v((TOK, SIG), F32),
        v((TOK, SIG), F32),
        v((TOK, SIG), BF16),
        v((TOK, SIG), BF16),
        v((TOK, SIG), BF16),
        v((2, STATE, SIG), BF16),
        v((2, HALF, SIG), BF16),
        v((8, 128), F32),
        v((8, 128), F32),
        v((CHIPS, 8, 128), F32),
        v((CHIPS, SIG), F32),
        v((8, SIG), F32),
        v((1, SIG), F32),
        v((2, HALF, SIG), BF16),
        v((2, CHIPS, ROWS, GW), BF16),
        v((2, CHIPS, ROWS, GW), BF16),
        v((2, HALF, SIG), BF16),
        v((2, HALF, SIG), BF16),
        v((2, STATE, SIG), BF16),
        v((TOK, SIG), F32),
        v((TOK, SIG), F32),
        v((TOK, 128), F32),
        v((TOK + 8, CH), F32),
        v((TOK, SIG), BF16),
        v((TOK, SIG), BF16),
        v((SIG, 128), BF16),
        v((8, SIG), F32),
        v((8, CH), F32),
        v((CTX, 8, 128), F32),
        v((DPS, 8, 128), F32),
        v((8, 128), F32),
        v((8, CH), F32),
        dma((7,)),
        dma((2,)),
        dma((2,)),
        dma((2,)),
        dma((CHIPS,)),
        dma((CHIPS,)),
        dma((2, GROUPS)),
        dma((2, GROUPS)),
        dma((2, CHIPS)),
        dma((2, CHIPS)),
        dma((2, CHIPS)),
        dma((2, CHIPS)),
        dma((2, GROUPS)),
        dma((2, GROUPS)),
        dma((2,)),
        dma((OWNERS,)),
        dma((CTX,)),
        dma((DPS,)),
        dma((DPS,)),
        dma((CTX,)),
        dma((CTX,)),
    ]


def body(conv_input, step_raw, log_decay, cotangent, conv_weight, conv_bias, skip_gain):
    vmem = pl.BlockSpec(memory_space=pltpu.VMEM)
    hbm = pl.BlockSpec(memory_space=pltpu.HBM)
    shapes = (
        jax.ShapeDtypeStruct((TOK, SIG), BF16),
        jax.ShapeDtypeStruct((TOK, CH), BF16),
        jax.ShapeDtypeStruct((HEADS, TOK), F32),
        jax.ShapeDtypeStruct((TAPS, CH), F32),
        jax.ShapeDtypeStruct((OWNERS, 128), F32),
        jax.ShapeDtypeStruct((1, HEADS), F32),
    )
    results = pl.pallas_call(
        kernel,
        out_shape=shapes,
        in_specs=[hbm] * 7,
        out_specs=[hbm] * 2 + [vmem] * 4,
        scratch_shapes=scratch(),
        compiler_params=pltpu.CompilerParams(
            collective_id=0, has_side_effects=True, vmem_limit_bytes=VMEM
        ),
    )(
        conv_input[0], step_raw[0].T, log_decay[0].T, cotangent[0],
        conv_weight, conv_bias.reshape(OWNERS, 128), skip_gain[None],
    )
    out, gin, sg, wg, bg, kg = pl.pallas_call(
        copy_kernel,
        out_shape=shapes,
        in_specs=[vmem] * 6,
        out_specs=[hbm] * 6,
        scratch_shapes=[pltpu.SemaphoreType.DMA((6,))],
    )(*results)
    return out[None], gin[None], sg.T[None], wg, bg.reshape(CH), kg[0]


def solution(mesh):
    split = P("dp", "ctx", None)
    return jax.shard_map(
        body,
        mesh=mesh,
        in_specs=(split, split, split, split, P(), P(), P()),
        out_specs=(split, split, split, P(), P(), P()),
        check_vma=False,
    )
```

time: 72.3 us -> 62.5 us (0.86)
  local copies, waits for them, and re-layouts: 6.79 us -> 0 us
  Pallas kernels: 63.9 us -> 61.7 us
    unnamed x19 -> x0, local copies, waits for them, and re-layouts: 6.07 us -> none
    pallas_call x1 -> x2, Pallas kernels: 63.9 us -> 61.7 us  [the longest x1 59.2 us: body(): pl.pallas_call(kernel, out_shape=shapes, in_specs=[hbm] * 7, out_specs=[h...]
where the time goes in v2:
time: 62.5 us; the launch traced here: 62.3 us
  Pallas kernels  61.7 us (99%)
  between operations  0.64 us (1%)
    pallas_call x1, Pallas kernels, body(): pl.pallas_call(kernel, out_shape=shapes, in_specs=[hbm] * 7, out_specs=[h...  59.2 us
    pallas_call x1, Pallas kernels, body(): pl.pallas_call(copy_kernel, out_shape=shapes, in_specs=[vmem] * 6, out_sp...  2.46 us

profile of v2, /device:TPU:1, one launch (start us, length us, event | category | flops | bytes accessed | tf_op | source)
XLA Modules:
  0.0 62.3 jit_solution(12896754341564979300)
XLA Ops:
  0.6 59.2 %shard_map.118 = (bf16[128,2560]{1,0:T(8,128)(2,1)}, bf16[128,2816]{1,0:T(8,128)(2,1)}, f32[40,128]{1,0:T(8,128)}, f32[4,2816]{1,0:T(4,128)}, f32[22,128]{1,0:T(8,128)}, /*index=5*/f32[1,40]{1,0:T(1,128)}) custom-call(bf16[128,2816]{1,0:T(8,128)(2,1)} %bitcast.17, f32[40,128]{1,0:T(8,128)} %bitcast.19, f32[40,128]{1,0:T(8,128)} %bitcast.20, ...), custom_call_target="tpu_custom_call" | custom-call | tf_op jit(solution)/shard_map/pallas_call | solution.py:630
  59.9 2.5 %shard_map.119 = (bf16[128,2560]{1,0:T(8,128)(2,1)}, bf16[128,2816]{1,0:T(8,128)(2,1)}, f32[40,128]{1,0:T(8,128)}, f32[4,2816]{1,0:T(4,128)}, f32[22,128]{1,0:T(8,128)}, /*index=5*/f32[1,40]{1,0:T(1,128)}) custom-call(bf16[128,2560]{1,0:T(8,128)(2,1)} %get-tuple-element.18.refs_0_, bf16[128,2816]{1,0:T(8,128)(2,1)} %get-tuple-element.19.refs_1_, ...), custom_call_target="tpu_custom_call" | custom-call | tf_op jit(solution)/shard_map/pallas_call | solution.py:643

commit v3 on v2

--- a/solution.py
+++ b/solution.py
@@ -22,8 +22,11 @@
 HALF = STATE // 2
 ROWS = 16
 OWNERS = CH // 128
-SPLIT_A = 6
-SPLIT_B = 13
+CUT_HALO = 6
+CUT_PAIR = 12
+CUT_SUMS = 3
+CUT_BACK = 8
+CUT_AHEAD = 14
 VMEM = 60 * 1024 * 1024
 LOG2E = 1.4426950408889634
 F32 = jnp.float32
@@ -43,12 +46,18 @@
     return hi, mid, low
 
 
-def loop(lo, hi, fn):
+def loop(lo, hi, fn, unroll=1):
+    whole = lo + (hi - lo) // unroll * unroll
+
     def step(i, carry):
-        fn(i)
+        for k in range(unroll):
+            fn(lo + i * unroll + k)
         return carry
 
-    lax.fori_loop(lo, hi, step, 0)
+    if whole > lo:
+        lax.fori_loop(0, (whole - lo) // unroll, step, 0)
+    for i in range(whole, hi):
+        fn(jnp.int32(i))
 
 
 def cols(i, width=128):
@@ -61,9 +70,9 @@
     out_ref, gin_ref, xb, cot_ref, w_ref, b_ref, skip_ref, raw_ref,
     xe, halo, act, dsil, ldp, stp, dst, dsx, stx, fsx, tex, tail, gst, sst,
     loc, prt, dec, decp, decg, dcx, coef, skx, tsum, rcv, res, inc, snd, fin,
-    oi, bi, run, gp, zhi, zlo, onehot, skp, part, ar1, ar2, sum1, tot,
-    in_sem, o_sem, h_sem, d_sem, dg_s, dg_r, p1_s, p1_r, a_s, a_r, b_s, b_r, p2_s, p2_r, g_sem,
-    r1_s, r1_r, r2_s, r2_r, r3_s, r3_r,
+    oi, bi, run, tmp, xsh, gp, zhi, zlo, onehot, skp, part, ar1, ar2, sum1, tot,
+    in_sem, o_sem, h_sem, d_sem, dg_s, p1_s, p1_r, a_s, a_r, b_s, b_r, p2_s, p2_r, g_sem,
+    r1_s, r2_s, r3_s,
 ):
     me = lax.axis_index("ctx")
     zed = lax.axis_index("dp")
@@ -82,6 +91,12 @@
             device_id={"ctx": ctx}, device_id_type=MESH,
         )
 
+    def left_all(ref, sem):
+        send(ref, ref, sem, sem, mate).wait_send()
+
+    def came_all(ref, sem):
+        send(ref, ref, sem, sem, mate).wait_recv()
+
     barrier = pltpu.get_barrier_semaphore()
 
     def greet_ctx(i):
@@ -122,20 +137,14 @@
     sums = sums_t.T
     decay = jnp.exp2(sums[TOK - 1 : TOK, :])
     dec[...] = jnp.broadcast_to(decay, (8, 128))
-    raw = raw_ref[...]
-    stp[0:HEADS, :] = jnp.maximum(raw, 0.0) + jnp.log1p(jnp.exp(-jnp.abs(raw)))
-    steps = stp[...].T
-
-    for h in range(HEADS):
-        dsx[:, 128 * h : 128 * h + 128] = jnp.broadcast_to(sums[:, h : h + 1], (TOK, 128))
     for g in range(BLOCKS):
         c = slice(128 * g, 128 * g + 128)
-        stx[:, c] = jnp.where(
-            left,
-            jnp.broadcast_to(steps[:, 2 * g : 2 * g + 1], (TOK, 128)),
-            jnp.broadcast_to(steps[:, 2 * g + 1 : 2 * g + 2], (TOK, 128)),
-        )
-        onehot[c, :] = (lanes == 2 * g + (rows >= WIDTH).astype(jnp.int32)).astype(BF16)
+        pair = [jnp.broadcast_to(sums[:, h : h + 1], (TOK, 128)) for h in (2 * g, 2 * g + 1)]
+        dsx[:, 256 * g : 256 * g + 128] = pair[0]
+        dsx[:, 256 * g + 128 : 256 * g + 256] = pair[1]
+        start = jnp.exp2(jnp.where(left, pair[0], pair[1]))
+        fsx[:, c] = start
+        gst[:, c] = (cot_ref[:, c].astype(F32) * start).astype(BF16)
 
     def expand(row, count):
         at = lax.broadcasted_iota(jnp.int32, (count, 128), 1) < WIDTH
@@ -148,25 +157,22 @@
             for g in range(BLOCKS)
         ]
 
-    for g, v in enumerate(expand(skip_ref[...], 1)):
-        skx[:, 128 * g : 128 * g + 128] = v
-
     def conv(j, r0, n):
         c = cols(j)
         pre = jnp.broadcast_to(b_ref[pl.ds(j, 1), :], (n, 128))
         for k in range(TAPS):
-            pre = pre + w_ref[k : k + 1, c] * xe[5 + k + r0 : 5 + k + r0 + n, c]
+            moved = xe[5 + k + r0 : 5 + k + r0 + n, c]
+            pre = pre + w_ref[k : k + 1, c] * moved
+            if k < TAPS - 1:
+                xsh[k, r0 : r0 + n, c] = moved
         sig = 1.0 / (1.0 + jnp.exp(-pre))
         act[r0 : r0 + n, c] = (pre * sig).astype(BF16)
         dsil[r0 : r0 + n, c] = sig * (1.0 + pre * (1.0 - sig))
 
-    def starts(g):
+    def ends(g):
         c = cols(g)
         ds = jnp.where(left, dsx[:, cols(2 * g)], dsx[:, cols(2 * g + 1)])
-        start = jnp.exp2(ds)
-        fsx[:, c] = start
         tex[:, c] = jnp.exp2(ds[TOK - 1 : TOK, :] - ds)
-        gst[:, c] = (cot_ref[:, c].astype(F32) * start).astype(BF16)
 
     def scaled(g, r0, n):
         c = cols(g)
@@ -183,10 +189,9 @@
 
     def later_signal(g):
         later_rows(g)
-        starts(g)
+        ends(g)
         scaled(g, ROWS, TOK - ROWS)
 
-    loop(0, BLOCKS, later_signal)
     loop(BLOCKS, BLOCKS + 2, later_rows)
 
     pl.semaphore_wait(barrier, CTX - 1 + DPS - 1)
@@ -196,6 +201,18 @@
     decay_copy = send(dec, decp, d_sem.at[0], d_sem.at[1], mate)
     decay_copy.start()
 
+    raw = raw_ref[...]
+    stp[0:HEADS, :] = jnp.maximum(raw, 0.0) + jnp.log1p(jnp.exp(-jnp.abs(raw)))
+    steps = stp[...].T
+    for g in range(BLOCKS):
+        c = slice(128 * g, 128 * g + 128)
+        stx[:, c] = jnp.where(
+            left,
+            jnp.broadcast_to(steps[:, 2 * g : 2 * g + 1], (TOK, 128)),
+            jnp.broadcast_to(steps[:, 2 * g + 1 : 2 * g + 2], (TOK, 128)),
+        )
+    loop(0, CUT_HALO, later_signal)
+
     decay_copy.wait()
     mine, other = dec[0:1, :], decp[0:1, :]
     decg[chip] = dec[...] * decp[...]
@@ -204,10 +221,7 @@
         return lax.rem(chip + i, CHIPS)
 
     def decay_out(q):
-        return send(decg.at[chip], decg.at[chip], dg_s.at[q], dg_r.at[chip], 2 * q + core)
-
-    def decay_in(q):
-        return send(decg.at[q], decg.at[q], dg_s.at[q], dg_r.at[q], 2 * q + core)
+        return send(decg.at[chip], decg.at[chip], dg_s.at[0], dg_s.at[1], 2 * q + core)
 
     loop(1, CHIPS, lambda i: decay_out(chip_at(i)).start())
     for g, (a, b) in enumerate(zip(expand(mine, 1), expand(other, 1))):
@@ -224,7 +238,7 @@
     def pair_one(k, j):
         c = cols(j, GW)
         there = pl.ds(pl.multiple_of(HALF * (1 - core), HALF), HALF)
-        return send(loc.at[k, there, c], prt.at[k, :, c], p1_s.at[k, j], p1_r.at[k, j], mate)
+        return send(loc.at[k, there, c], prt.at[k, :, c], p1_s.at[k], p1_r.at[k, j], mate)
 
     readout_t = readout.T
 
@@ -235,11 +249,6 @@
 
     loop(0, GROUPS, local_adjoint)
 
-    def early_rows(g):
-        conv(g, 0, ROWS)
-        scaled(g, 0, ROWS)
-
-    loop(0, BLOCKS, early_rows)
     inject_t = inject.T
 
     def local_state(j):
@@ -256,12 +265,7 @@
         return ref.at[k, r, cols(lax.rem(q, 4), GW)]
 
     def state_out(k, q):
-        return send(
-            piece(tsum, k, q), rcv.at[k, chip], a_s.at[k, q], a_r.at[k, chip], 2 * q + core
-        )
-
-    def state_in(k, q):
-        return send(piece(tsum, k, q), rcv.at[k, q], a_s.at[k, q], a_r.at[k, q], 2 * q + core)
+        return send(piece(tsum, k, q), rcv.at[k, chip], a_s.at[k], a_r.at[k], 2 * q + core)
 
     def chip_sums(k):
         def group(j):
@@ -288,9 +292,15 @@
         loop(0, GROUPS, group)
         rcv[k, chip] = tsum[k, own_rows, qc]
 
+    def early_rows(g):
+        conv(g, 0, ROWS)
+        scaled(g, 0, ROWS)
+
+    loop(CUT_HALO, CUT_PAIR, later_signal)
     chip_sums(1)
+    loop(CUT_PAIR, BLOCKS, later_signal)
+    loop(0, BLOCKS, early_rows, 2)
     loop(0, GROUPS, local_state)
-    chip_sums(0)
 
     scores = dot(readout, inject, ((1,), (1,)))
     scores_t = dot(inject, readout, ((1,), (1,)))
@@ -317,34 +327,42 @@
         run[...] += fades[0] * inner[:, :128] + fades[1] * inner[:, 128:]
         skp[:, c] = jnp.sum((act[:, c].astype(F32) * t.astype(F32)).reshape(TOK // 8, 8, 128), axis=0)
 
-    loop(0, SPLIT_A, intra)
-
-    loop(1, CHIPS, lambda i: decay_in(chip_at(i)).wait_recv())
+    loop(0, CUT_SUMS, intra)
+    chip_sums(0)
+    for g, v in enumerate(expand(skip_ref[...], 1)):
+        skx[:, 128 * g : 128 * g + 128] = v
+        onehot[128 * g : 128 * g + 128, :] = (
+            lanes == 2 * g + (rows >= WIDTH).astype(jnp.int32)
+        ).astype(BF16)
+    loop(CUT_SUMS, CUT_BACK, intra)
+
+    came_all(decg.at[pl.ds(0, CHIPS - 1)], dg_s.at[1])
     for g, v in enumerate(expand(decg[:, 0, :], CHIPS)):
         dcx[:, 128 * g : 128 * g + 128] = v
 
     def result_out(k, q):
-        return send(res.at[k, q], piece(inc, k, chip), b_s.at[k, q], b_r.at[k, chip], 2 * q + core)
-
-    def result_in(k, q):
-        return send(res.at[k, q], piece(inc, k, q), b_s.at[k, q], b_r.at[k, q], 2 * q + core)
+        return send(res.at[k, q], piece(inc, k, chip), b_s.at[k], b_r.at[k, quarter], 2 * q + core)
 
     def scan(k):
-        loop(1, CHIPS, lambda i: state_in(k, chip_at(i)).wait_recv())
+        came_all(rcv.at[k, pl.ds(0, CHIPS - 1)], a_r.at[k])
 
         def step(i, carry):
             q = i if k == 0 else CHIPS - 1 - i
             res[k, q] = carry.astype(BF16)
+
+            @pl.when(q != chip)
+            def _():
+                result_out(k, q).start()
+
             return dcx[pl.ds(q, 1), qc] * carry + rcv[k, q].astype(F32)
 
         lax.fori_loop(0, CHIPS, step, jnp.zeros((ROWS, GW), F32))
-        loop(1, CHIPS, lambda i: result_out(k, chip_at(i)).start())
         inc[k, own_rows, qc] = res[k, chip]
 
     scan(1)
-    loop(SPLIT_A, SPLIT_B, intra)
+    loop(CUT_BACK, CUT_AHEAD, intra)
     scan(0)
-    loop(SPLIT_B, BLOCKS, intra)
+    loop(CUT_AHEAD, BLOCKS, intra)
 
     skip_heads = sum(dot(v, onehot[...]) for v in split3(skp[...]))
     mix_total = jnp.where(lower, run[...], 0.0).astype(BF16)
@@ -355,19 +373,20 @@
 
     def pair_two(k, j):
         c = cols(j, GW)
-        return send(snd.at[k, :, c], fin.at[k, here, c], p2_s.at[k, j], p2_r.at[k, j], mate)
+        return send(snd.at[k, :, c], fin.at[k, here, c], p2_s.at[k], p2_r.at[k, j], mate)
 
     def spread(k):
         def group(j):
-            def arrive(r):
-                q = 4 * r + j
-
-                @pl.when(q != chip)
-                def _():
-                    result_in(k, q).wait_recv()
-
-            loop(0, 4, arrive)
             c = cols(j, GW)
+
+            @pl.when(j == quarter)
+            def _():
+                came_all(inc.at[k, pl.ds(0, HALF - ROWS), c], b_r.at[k, j])
+
+            @pl.when(j != quarter)
+            def _():
+                came_all(inc.at[k, :, c], b_r.at[k, j])
+
             came = inc[k, :, c]
             wide = came.astype(F32)
             near = (coef[0:1, c] * wide + loc[k, here, c].astype(F32)).astype(BF16)
@@ -385,10 +404,7 @@
     spread(1)
 
     def tile_out(j):
-        return send(part.at[:, cols(j)], ar1.at[me], r1_s.at[j], r1_r.at[me], j)
-
-    def tile_in(i):
-        return send(part.at[:, cols(0)], ar1.at[i], r1_s.at[0], r1_r.at[i], i)
+        return send(part.at[:, cols(j)], ar1.at[me], r1_s.at[0], r1_s.at[1], j)
 
     def each_other(i, fn):
         @pl.when(i != me)
@@ -400,15 +416,16 @@
         grad = grad_act * dsil[:, c]
         gp[0:TOK, c] = grad
         for k in range(TAPS):
-            part[k : k + 1, c] = jnp.sum(grad * xe[5 + k : 5 + k + TOK, c], axis=0, keepdims=True)
+            moved = xe[8:, c] if k == TAPS - 1 else xsh[k, :, c]
+            part[k : k + 1, c] = jnp.sum(grad * moved, axis=0, keepdims=True)
         part[4:5, c] = jnp.sum(grad, axis=0, keepdims=True)
         each_other(j, lambda j: tile_out(j).start())
 
-    def finish(g):
+    def finish(g, i):
         c = cols(g)
         s = act[:, c].astype(F32)
         t = cot_ref[:, c].astype(F32)
-        back = bi[:, c] + tex[:, c] * dot(inject, fin[1, :, c])
+        back = bi[:, c] + tex[:, c] * tmp[:, cols(i)]
         z = s * back
         z_hi = z.astype(BF16)
         zhi[:, c] = z_hi
@@ -417,7 +434,8 @@
 
     def finish_group(j):
         pair_two(1, j).wait_recv()
-        loop(0, GB, lambda i: finish(j * GB + i))
+        tmp[...] = dot(inject, fin[1, :, cols(j, GW)])
+        loop(0, GB, lambda i: finish(j * GB + i, i))
 
     loop(0, GROUPS, finish_group)
     finish_rows(BLOCKS, grad_inject + dot(tail[...], fin[1], ((1,), (1,))))
@@ -428,40 +446,34 @@
     grad_halo = send(gp.at[pl.ds(0, 8), :], gp.at[pl.ds(TOK, 8), :], g_sem.at[0], g_sem.at[1], prv)
     grad_halo.start()
 
-    def output(g):
+    def output(g, i):
         c = cols(g)
-        out = oi[:, c] + fsx[:, c] * dot(readout, fin[0, :, c]) + skx[:, c] * act[:, c].astype(F32)
+        out = oi[:, c] + fsx[:, c] * tmp[:, cols(i)] + skx[:, c] * act[:, c].astype(F32)
         out_ref[:, c] = out.astype(BF16)
 
-    loop(0, BLOCKS, output)
+    def output_group(j):
+        tmp[...] = dot(readout, fin[0, :, cols(j, GW)])
+        loop(0, GB, lambda i: output(j * GB + i, i))
+
+    loop(0, GROUPS, output_group)
     out_copy = pltpu.make_async_copy(out_ref, out_hbm, o_sem.at[0])
     out_copy.start()
 
     def dp_out(i):
         z = lax.rem(zed + i, DPS)
         return pltpu.make_async_remote_copy(
-            src_ref=sum1, dst_ref=ar2.at[zed], send_sem=r2_s.at[z], recv_sem=r2_r.at[zed],
+            src_ref=sum1, dst_ref=ar2.at[zed], send_sem=r2_s.at[0], recv_sem=r2_s.at[1],
             device_id={"dp": z}, device_id_type=MESH,
         )
 
-    def dp_in(i):
-        z = lax.rem(zed + i, DPS)
-        return pltpu.make_async_remote_copy(
-            src_ref=sum1, dst_ref=ar2.at[z], send_sem=r2_s.at[z], recv_sem=r2_r.at[z],
-            device_id={"dp": z}, device_id_type=MESH,
-        )
-
     def total_out(i):
-        return send(tot.at[:, cols(me)], tot.at[:, cols(me)], r3_s.at[i], r3_r.at[me], i)
-
-    def total_in(i):
-        return send(tot.at[:, cols(i)], tot.at[:, cols(i)], r3_s.at[i], r3_r.at[i], i)
+        return send(tot.at[:, cols(me)], tot.at[:, cols(me)], r3_s.at[0], r3_s.at[1], i)
 
     owner = me < OWNERS
 
     @pl.when(owner)
     def _():
-        loop(0, CTX, lambda i: each_other(i, lambda i: tile_in(i).wait_recv()))
+        came_all(ar1.at[pl.ds(0, CTX - 1)], r1_s.at[1])
         ar1[me] = part[:, cols(me)]
         sum1[...] = jnp.sum(ar1[...], axis=0)
         loop(1, DPS, lambda i: dp_out(i).start())
@@ -485,7 +497,7 @@
 
     @pl.when(owner)
     def _():
-        loop(1, DPS, lambda i: dp_in(i).wait_recv())
+        came_all(ar2.at[pl.ds(0, DPS - 1)], r2_s.at[1])
         ar2[zed] = sum1[...]
         tot[:, cols(me)] = jnp.sum(ar2[...], axis=0)
         loop(0, CTX, lambda i: each_other(i, lambda i: total_out(i).start()))
@@ -497,23 +509,26 @@
     halo_copy.wait_send()
     grad_halo.wait_send()
 
-    def pairs_done(j):
-        for k in range(2):
-            pair_one(k, j).wait_send()
-            pair_two(k, j).wait_send()
-
-    def chips_done(i):
-        q = chip_at(i)
-        decay_out(q).wait_send()
-        for k in range(2):
-            state_out(k, q).wait_send()
-            result_out(k, q).wait_send()
-
-    loop(0, GROUPS, pairs_done)
-    loop(1, CHIPS, chips_done)
-    loop(0, OWNERS, lambda j: each_other(j, lambda j: tile_out(j).wait_send()))
-
-    loop(0, OWNERS, lambda i: each_other(i, lambda i: total_in(i).wait_recv()))
+    left_all(decg.at[pl.ds(0, CHIPS - 1)], dg_s.at[0])
+    for k in range(2):
+        left_all(tsum.at[k], p1_s.at[k])
+        left_all(tsum.at[k], p2_s.at[k])
+        left_all(rcv.at[k, pl.ds(0, CHIPS - 1)], a_s.at[k])
+        left_all(rcv.at[k, pl.ds(0, CHIPS - 1)], b_s.at[k])
+
+    @pl.when(owner)
+    def _():
+        some = tot.at[:, pl.ds(0, CH - 128)]
+        left_all(some, r1_s.at[0])
+        left_all(ar2.at[pl.ds(0, DPS - 1)], r2_s.at[0])
+        left_all(ar1.at[pl.ds(0, CTX - 1)], r3_s.at[0])
+        came_all(some, r3_s.at[1])
+
+    @pl.when(jnp.logical_not(owner))
+    def _():
+        left_all(tot, r1_s.at[0])
+        came_all(tot, r3_s.at[1])
+
     wg_ref[...] = tot[0:TAPS, :]
     for j in range(OWNERS):
         bg_ref[j : j + 1, :] = tot[4:5, 128 * j : 128 * j + 128]
@@ -521,21 +536,18 @@
     out_copy.wait()
     gin_copy.wait()
 
-    @pl.when(owner)
-    def _():
-        loop(1, DPS, lambda i: dp_out(i).wait_send())
-        loop(0, CTX, lambda i: each_other(i, lambda i: total_out(i).wait_send()))
-
 
 def copy_kernel(*refs):
-    n = (len(refs) - 1) // 2
-    sem = refs[-1]
-    copies = [
-        pltpu.make_async_copy(refs[i], refs[n + i], sem.at[i]) for i in range(n)
-    ]
-    for copy in copies:
+    n = (len(refs) - 2) // 3
+    src, dst, via, (isem, osem) = refs[:n], refs[n : 2 * n], refs[2 * n : 3 * n], refs[3 * n :]
+    first = [pltpu.make_async_copy(src[i], via[i], isem.at[i]) for i in range(n)]
+    second = [pltpu.make_async_copy(via[i], dst[i], osem.at[i]) for i in range(n)]
+    for copy in first:
         copy.start()
-    for copy in copies:
+    for a, b in zip(first, second):
+        a.wait()
+        b.start()
+    for copy in second:
         copy.wait()
 
 
@@ -582,6 +594,8 @@
         v((TOK, SIG), F32),
         v((TOK, SIG), F32),
         v((TOK, 128), F32),
+        v((TOK, GW), F32),
+        v((TAPS - 1, TOK, CH), F32),
         v((TOK + 8, CH), F32),
         v((TOK, SIG), BF16),
         v((TOK, SIG), BF16),
@@ -596,23 +610,19 @@
         dma((2,)),
         dma((2,)),
         dma((2,)),
-        dma((CHIPS,)),
-        dma((CHIPS,)),
+        dma((2,)),
+        dma((2,)),
         dma((2, GROUPS)),
+        dma((2,)),
+        dma((2,)),
+        dma((2,)),
         dma((2, GROUPS)),
-        dma((2, CHIPS)),
-        dma((2, CHIPS)),
-        dma((2, CHIPS)),
-        dma((2, CHIPS)),
+        dma((2,)),
         dma((2, GROUPS)),
-        dma((2, GROUPS)),
-        dma((2,)),
-        dma((OWNERS,)),
-        dma((CTX,)),
-        dma((DPS,)),
-        dma((DPS,)),
-        dma((CTX,)),
-        dma((CTX,)),
+        dma((2,)),
+        dma((2,)),
+        dma((2,)),
+        dma((2,)),
     ]
 
 
@@ -643,9 +653,11 @@
     out, gin, sg, wg, bg, kg = pl.pallas_call(
         copy_kernel,
         out_shape=shapes,
-        in_specs=[vmem] * 6,
+        in_specs=[hbm] * 6,
         out_specs=[hbm] * 6,
-        scratch_shapes=[pltpu.SemaphoreType.DMA((6,))],
+        scratch_shapes=[pltpu.VMEM(a.shape, a.dtype) for a in shapes]
+        + [pltpu.SemaphoreType.DMA((6,))] * 2,
+        compiler_params=pltpu.CompilerParams(vmem_limit_bytes=VMEM),
     )(*results)
     return out[None], gin[None], sg.T[None], wg, bg.reshape(CH), kg[0]
 

time: 62.5 us -> 54.1 us (0.87)
  Pallas kernels: 61.7 us -> 53.3 us
    pallas_call x1, Pallas kernels: 59.2 us -> 51 us  [body(): pl.pallas_call(kernel, out_shape=shapes, in_specs=[hbm] * 7, out_specs=[h...]
where the time goes in v3:
time: 54.1 us; the launch traced here: 54 us
  Pallas kernels  53.3 us (99%)
  between operations  0.64 us (1%)
    pallas_call x1, Pallas kernels, body(): pl.pallas_call(kernel, out_shape=shapes, in_specs=[hbm] * 7, out_specs=[h...  51 us
    pallas_call x1, Pallas kernels, body(): pl.pallas_call(copy_kernel, out_shape=shapes, in_specs=[hbm] * 6, out_spe...  2.28 us

profile of v3, /device:TPU:1, one launch (start us, length us, event | category | flops | bytes accessed | tf_op | source)
XLA Modules:
  0.0 54.0 jit_solution(8791935732308844637)
XLA Ops:
  0.6 51.0 %shard_map.118 = (bf16[128,2560]{1,0:T(8,128)(2,1)}, bf16[128,2816]{1,0:T(8,128)(2,1)}, f32[40,128]{1,0:T(8,128)}, f32[4,2816]{1,0:T(4,128)}, f32[22,128]{1,0:T(8,128)}, /*index=5*/f32[1,40]{1,0:T(1,128)}) custom-call(bf16[128,2816]{1,0:T(8,128)(2,1)} %bitcast.17, f32[40,128]{1,0:T(8,128)} %bitcast.19, f32[40,128]{1,0:T(8,128)} %bitcast.20, ...), custom_call_target="tpu_custom_call" | custom-call | tf_op jit(solution)/shard_map/pallas_call | solution.py:640
  51.7 2.3 %shard_map.119 = (bf16[128,2560]{1,0:T(8,128)(2,1)}, bf16[128,2816]{1,0:T(8,128)(2,1)}, f32[40,128]{1,0:T(8,128)}, f32[4,2816]{1,0:T(4,128)}, f32[22,128]{1,0:T(8,128)}, /*index=5*/f32[1,40]{1,0:T(1,128)}) custom-call(bf16[128,2560]{1,0:T(8,128)(2,1)} %get-tuple-element.18.refs_0_, bf16[128,2816]{1,0:T(8,128)(2,1)} %get-tuple-element.19.refs_1_, ...), custom_call_target="tpu_custom_call" | custom-call | tf_op jit(solution)/shard_map/pallas_call | solution.py:653

commit v4 on v3

--- a/solution.py
+++ b/solution.py
@@ -27,7 +27,7 @@
 CUT_SUMS = 3
 CUT_BACK = 8
 CUT_AHEAD = 14
-VMEM = 60 * 1024 * 1024
+VMEM = 48 * 1024 * 1024
 LOG2E = 1.4426950408889634
 F32 = jnp.float32
 BF16 = jnp.bfloat16
@@ -66,12 +66,12 @@
 
 def kernel(
     x_hbm, raw_hbm, ld_hbm, cot_hbm, w_hbm, b_hbm, skip_hbm,
-    out_hbm, gin_hbm, sg_ref, wg_ref, bg_ref, kg_ref,
-    out_ref, gin_ref, xb, cot_ref, w_ref, b_ref, skip_ref, raw_ref,
+    out_ref, gin_ref, sg_ref, wg_ref, bg_ref, kg_ref,
+    xb, cot_ref, w_ref, b_ref, skip_ref, raw_ref,
     xe, halo, act, dsil, ldp, stp, dst, dsx, stx, fsx, tex, tail, gst, sst,
     loc, prt, dec, decp, decg, dcx, coef, skx, tsum, rcv, res, inc, snd, fin,
     oi, bi, run, tmp, xsh, gp, zhi, zlo, onehot, skp, part, ar1, ar2, sum1, tot,
-    in_sem, o_sem, h_sem, d_sem, dg_s, p1_s, p1_r, a_s, a_r, b_s, b_r, p2_s, p2_r, g_sem,
+    in_sem, h_sem, d_sem, dg_s, p1_s, p1_r, a_s, a_r, b_s, b_r, p2_s, p2_r, g_sem,
     r1_s, r2_s, r3_s,
 ):
     me = lax.axis_index("ctx")
@@ -90,6 +90,10 @@
             src_ref=src, dst_ref=dst, send_sem=ssem, recv_sem=rsem,
             device_id={"ctx": ctx}, device_id_type=MESH,
         )
+
+    def turned(i, own):
+        away = jnp.where(i == 0, 2, jnp.where(i == 1, 1, jnp.where(i == 2, 3, 0)))
+        return lax.rem(own + away, 4)
 
     def left_all(ref, sem):
         send(ref, ref, sem, sem, mate).wait_send()
@@ -211,7 +215,7 @@
             jnp.broadcast_to(steps[:, 2 * g : 2 * g + 1], (TOK, 128)),
             jnp.broadcast_to(steps[:, 2 * g + 1 : 2 * g + 2], (TOK, 128)),
         )
-    loop(0, CUT_HALO, later_signal)
+    loop(0, CUT_HALO, later_signal, 2)
 
     decay_copy.wait()
     mine, other = dec[0:1, :], decp[0:1, :]
@@ -242,7 +246,8 @@
 
     readout_t = readout.T
 
-    def local_adjoint(j):
+    def local_adjoint(i):
+        j = turned(i, quarter)
         c = cols(j, GW)
         loc[1, :, c] = dot(readout_t, gst[:, c]).astype(BF16)
         pair_one(1, j).start()
@@ -251,7 +256,8 @@
 
     inject_t = inject.T
 
-    def local_state(j):
+    def local_state(i):
+        j = turned(i, quarter)
         c = cols(j, GW)
         loc[0, :, c] = dot(inject_t, tail[:, c]).astype(BF16)
         pair_one(0, j).start()
@@ -268,7 +274,8 @@
         return send(piece(tsum, k, q), rcv.at[k, chip], a_s.at[k], a_r.at[k], 2 * q + core)
 
     def chip_sums(k):
-        def group(j):
+        def group(i):
+            j = turned(i, quarter)
             pair_one(k, j).wait_recv()
             c = cols(j, GW)
             a, b = coef[0:1, c], coef[1:2, c]
@@ -281,7 +288,7 @@
             tsum[k, :, c] = total.astype(BF16)
 
             def out(r):
-                q = 4 * r + j
+                q = 4 * turned(r, band) + j
 
                 @pl.when(q != chip)
                 def _():
@@ -296,9 +303,9 @@
         conv(g, 0, ROWS)
         scaled(g, 0, ROWS)
 
-    loop(CUT_HALO, CUT_PAIR, later_signal)
+    loop(CUT_HALO, CUT_PAIR, later_signal, 2)
     chip_sums(1)
-    loop(CUT_PAIR, BLOCKS, later_signal)
+    loop(CUT_PAIR, BLOCKS, later_signal, 2)
     loop(0, BLOCKS, early_rows, 2)
     loop(0, GROUPS, local_state)
 
@@ -327,14 +334,14 @@
         run[...] += fades[0] * inner[:, :128] + fades[1] * inner[:, 128:]
         skp[:, c] = jnp.sum((act[:, c].astype(F32) * t.astype(F32)).reshape(TOK // 8, 8, 128), axis=0)
 
-    loop(0, CUT_SUMS, intra)
+    loop(0, CUT_SUMS, intra, 2)
     chip_sums(0)
     for g, v in enumerate(expand(skip_ref[...], 1)):
         skx[:, 128 * g : 128 * g + 128] = v
         onehot[128 * g : 128 * g + 128, :] = (
             lanes == 2 * g + (rows >= WIDTH).astype(jnp.int32)
         ).astype(BF16)
-    loop(CUT_SUMS, CUT_BACK, intra)
+    loop(CUT_SUMS, CUT_BACK, intra, 2)
 
     came_all(decg.at[pl.ds(0, CHIPS - 1)], dg_s.at[1])
     for g, v in enumerate(expand(decg[:, 0, :], CHIPS)):
@@ -349,20 +356,21 @@
         def step(i, carry):
             q = i if k == 0 else CHIPS - 1 - i
             res[k, q] = carry.astype(BF16)
-
-            @pl.when(q != chip)
-            def _():
-                result_out(k, q).start()
-
             return dcx[pl.ds(q, 1), qc] * carry + rcv[k, q].astype(F32)
 
         lax.fori_loop(0, CHIPS, step, jnp.zeros((ROWS, GW), F32))
+
+        def out(i):
+            q = 4 * turned(i // 4, band) + turned(lax.rem(i, 4), quarter)
+            result_out(k, q).start()
+
+        loop(0, CHIPS - 1, out)
         inc[k, own_rows, qc] = res[k, chip]
 
     scan(1)
-    loop(CUT_BACK, CUT_AHEAD, intra)
+    loop(CUT_BACK, CUT_AHEAD, intra, 2)
     scan(0)
-    loop(CUT_AHEAD, BLOCKS, intra)
+    loop(CUT_AHEAD, BLOCKS, intra, 2)
 
     skip_heads = sum(dot(v, onehot[...]) for v in split3(skp[...]))
     mix_total = jnp.where(lower, run[...], 0.0).astype(BF16)
@@ -376,7 +384,8 @@
         return send(snd.at[k, :, c], fin.at[k, here, c], p2_s.at[k], p2_r.at[k, j], mate)
 
     def spread(k):
-        def group(j):
+        def group(i):
+            j = lax.rem(quarter + i, 4)
             c = cols(j, GW)
 
             @pl.when(j == quarter)
@@ -419,7 +428,6 @@
             moved = xe[8:, c] if k == TAPS - 1 else xsh[k, :, c]
             part[k : k + 1, c] = jnp.sum(grad * moved, axis=0, keepdims=True)
         part[4:5, c] = jnp.sum(grad, axis=0, keepdims=True)
-        each_other(j, lambda j: tile_out(j).start())
 
     def finish(g, i):
         c = cols(g)
@@ -432,16 +440,20 @@
         zlo[:, c] = (z - z_hi.astype(F32)).astype(BF16)
         finish_rows(g, stx[:, c] * back + skx[:, c] * t)
 
-    def finish_group(j):
+    def finish_group(i):
+        j = lax.rem(quarter + i, 4)
         pair_two(1, j).wait_recv()
         tmp[...] = dot(inject, fin[1, :, cols(j, GW)])
-        loop(0, GB, lambda i: finish(j * GB + i, i))
+        loop(0, GB, lambda i: finish(j * GB + i, i), GB)
+        loop(0, GB, lambda i: each_other(j * GB + i, lambda t: tile_out(t).start()))
 
     loop(0, GROUPS, finish_group)
     finish_rows(BLOCKS, grad_inject + dot(tail[...], fin[1], ((1,), (1,))))
+    each_other(BLOCKS, lambda j: tile_out(j).start())
     spread(0)
     loop(0, GROUPS, lambda j: pair_two(0, j).wait_recv())
     finish_rows(BLOCKS + 1, grad_readout + dot(gst[...], fin[0], ((1,), (1,))))
+    each_other(OWNERS - 1, lambda j: tile_out(j).start())
 
     grad_halo = send(gp.at[pl.ds(0, 8), :], gp.at[pl.ds(TOK, 8), :], g_sem.at[0], g_sem.at[1], prv)
     grad_halo.start()
@@ -456,8 +468,6 @@
         loop(0, GB, lambda i: output(j * GB + i, i))
 
     loop(0, GROUPS, output_group)
-    out_copy = pltpu.make_async_copy(out_ref, out_hbm, o_sem.at[0])
-    out_copy.start()
 
     def dp_out(i):
         z = lax.rem(zed + i, DPS)
@@ -500,11 +510,9 @@
         came_all(ar2.at[pl.ds(0, DPS - 1)], r2_s.at[1])
         ar2[zed] = sum1[...]
         tot[:, cols(me)] = jnp.sum(ar2[...], axis=0)
-        loop(0, CTX, lambda i: each_other(i, lambda i: total_out(i).start()))
+        loop(1, CTX, lambda i: total_out(lax.rem(me + i, CTX)).start())
 
     loop(CH // 256, CH // 128, input_grad)
-    gin_copy = pltpu.make_async_copy(gin_ref, gin_hbm, o_sem.at[1])
-    gin_copy.start()
 
     halo_copy.wait_send()
     grad_halo.wait_send()
@@ -533,21 +541,14 @@
     for j in range(OWNERS):
         bg_ref[j : j + 1, :] = tot[4:5, 128 * j : 128 * j + 128]
     kg_ref[...] = tot[5:6, 0:HEADS]
-    out_copy.wait()
-    gin_copy.wait()
 
 
 def copy_kernel(*refs):
-    n = (len(refs) - 2) // 3
-    src, dst, via, (isem, osem) = refs[:n], refs[n : 2 * n], refs[2 * n : 3 * n], refs[3 * n :]
-    first = [pltpu.make_async_copy(src[i], via[i], isem.at[i]) for i in range(n)]
-    second = [pltpu.make_async_copy(via[i], dst[i], osem.at[i]) for i in range(n)]
-    for copy in first:
+    n = len(refs) // 2
+    copies = [pltpu.make_async_copy(refs[i], refs[n + i], refs[-1].at[i]) for i in range(n)]
+    for copy in copies:
         copy.start()
-    for a, b in zip(first, second):
-        a.wait()
-        b.start()
-    for copy in second:
+    for copy in copies:
         copy.wait()
 
 
@@ -555,8 +556,6 @@
     v = pltpu.VMEM
     dma = pltpu.SemaphoreType.DMA
     return [
-        v((TOK, SIG), BF16),
-        v((TOK, CH), BF16),
         v((TOK, CH), BF16),
         v((TOK, SIG), BF16),
         v((TAPS, CH), F32),
@@ -611,7 +610,6 @@
         dma((2,)),
         dma((2,)),
         dma((2,)),
-        dma((2,)),
         dma((2, GROUPS)),
         dma((2,)),
         dma((2,)),
@@ -639,26 +637,24 @@
     )
     results = pl.pallas_call(
         kernel,
-        out_shape=shapes,
+        out_shape=[pltpu.VMEM(a.shape, a.dtype) for a in shapes],
         in_specs=[hbm] * 7,
-        out_specs=[hbm] * 2 + [vmem] * 4,
+        out_specs=[vmem] * 6,
         scratch_shapes=scratch(),
         compiler_params=pltpu.CompilerParams(
             collective_id=0, has_side_effects=True, vmem_limit_bytes=VMEM
         ),
-    )(
+    )(*(pltpu.with_memory_space_constraint(a, pltpu.HBM) for a in (
         conv_input[0], step_raw[0].T, log_decay[0].T, cotangent[0],
         conv_weight, conv_bias.reshape(OWNERS, 128), skip_gain[None],
-    )
+    )))
     out, gin, sg, wg, bg, kg = pl.pallas_call(
         copy_kernel,
         out_shape=shapes,
-        in_specs=[hbm] * 6,
+        in_specs=[vmem] * 6,
         out_specs=[hbm] * 6,
-        scratch_shapes=[pltpu.VMEM(a.shape, a.dtype) for a in shapes]
-        + [pltpu.SemaphoreType.DMA((6,))] * 2,
-        compiler_params=pltpu.CompilerParams(vmem_limit_bytes=VMEM),
-    )(*results)
+        scratch_shapes=[pltpu.SemaphoreType.DMA((6,))],
+    )(*(pltpu.with_memory_space_constraint(a, pltpu.VMEM) for a in results))
     return out[None], gin[None], sg.T[None], wg, bg.reshape(CH), kg[0]
 
 

time: 54.1 us -> 50.9 us (0.941)
  Pallas kernels: 53.3 us -> 50.2 us
    pallas_call x2, Pallas kernels: 53.3 us -> 50.2 us  [the longest x1 49 us: body(): pl.pallas_call(kernel, out_shape=[pltpu.VMEM(a.shape, a.dtype) for a in s...]
where the time goes in v4:
time: 50.9 us; the launch traced here: 50.8 us
  Pallas kernels  50.2 us (99%)
  between operations  0.64 us (1%)
    pallas_call x1, Pallas kernels, body(): pl.pallas_call(kernel, out_shape=[pltpu.VMEM(a.shape, a.dtype) for a in s...  49 us
    pallas_call x1, Pallas kernels, body(): pl.pallas_call(copy_kernel, out_shape=shapes, in_specs=[vmem] * 6, out_sp...  1.14 us

profile of v4, /device:TPU:1, one launch (start us, length us, event | category | flops | bytes accessed | tf_op | source)
XLA Modules:
  0.0 50.8 jit_solution(15215801431602087933)
XLA Ops:
  0.6 49.0 %shard_map.118 = (bf16[128,2560]{1,0:T(8,128)(2,1)S(1)}, bf16[128,2816]{1,0:T(8,128)(2,1)S(1)}, f32[40,128]{1,0:T(8,128)S(1)}, f32[4,2816]{1,0:T(4,128)S(1)}, f3...) custom-call(bf16[128,2816]{1,0:T(8,128)(2,1)} %bitcast.17, f32[40,128]{1,0:T(8,128)} %bitcast.19, f32[40,128]{1,0:T(8,128)} %bitcast.20, ...), custom_call_target="tpu_custom_call" | custom-call | tf_op jit(solution)/shard_map/pallas_call | solution.py:638
  49.7 1.1 %shard_map.119 = (bf16[128,2560]{1,0:T(8,128)(2,1)}, bf16[128,2816]{1,0:T(8,128)(2,1)}, f32[40,128]{1,0:T(8,128)}, f32[4,2816]{1,0:T(4,128)}, f32[22,128]{1,0:T(8,128)}, /*index=5*/f32[1,40]{1,0:T(1,128)}) custom-call(bf16[128,2560]{1,0:T(8,128)(2,1)S(1)} %get-tuple-element.18.refs_0_, bf16[128,2816]{1,0:T(8,128)(2,1)S(1)} %get-tuple-element.19.refs_1_, ...), custom_call_target="tpu_custom_call" | custom-call | tf_op jit(solution)/shard_map/pallas_call | solution.py:651

commit v5 on v4

--- a/solution.py
+++ b/solution.py
@@ -22,8 +22,8 @@
 HALF = STATE // 2
 ROWS = 16
 OWNERS = CH // 128
-CUT_HALO = 6
-CUT_PAIR = 12
+CUT_HALO = 4
+CUT_PAIR = 10
 CUT_SUMS = 3
 CUT_BACK = 8
 CUT_AHEAD = 14
@@ -91,15 +91,23 @@
             device_id={"ctx": ctx}, device_id_type=MESH,
         )
 
+    def left_all(ref, sem):
+        send(ref, ref, sem, sem, mate).wait_send()
+
+    def came_all(ref, sem):
+        send(ref, ref, sem, sem, mate).wait_recv()
+
     def turned(i, own):
         away = jnp.where(i == 0, 2, jnp.where(i == 1, 1, jnp.where(i == 2, 3, 0)))
         return lax.rem(own + away, 4)
 
-    def left_all(ref, sem):
-        send(ref, ref, sem, sem, mate).wait_send()
-
-    def came_all(ref, sem):
-        send(ref, ref, sem, sem, mate).wait_recv()
+    def far_first(i):
+        q = 4 * turned(i // 8, band) + turned(lax.rem(i // 2, 4), quarter)
+        return 2 * q + lax.rem(core + 1 + i, 2)
+
+    def far_dp(i):
+        half = (i + 1) // 2
+        return lax.rem(zed + 4 + jnp.where(lax.rem(i, 2) == 0, half, DPS - half), DPS)
 
     barrier = pltpu.get_barrier_semaphore()
 
@@ -133,14 +141,16 @@
     ldp[HEADS:, :] = jnp.zeros((128 - HEADS, TOK), F32)
     stp[...] = jnp.zeros((128, TOK), F32)
     xe[0:8, :] = jnp.zeros((8, CH), F32)
-    for copy in fetch:
-        copy.wait()
-
-    sums_t = dot(ldp[...] * LOG2E, (rows <= lanes).astype(F32), precision=lax.Precision.HIGHEST)
+    fetch[0].wait()
+
+    ones = (rows <= lanes).astype(BF16)
+    sums_t = sum(dot(v, ones) for v in split3(ldp[...] * LOG2E))
     dst[...] = sums_t
     sums = sums_t.T
     decay = jnp.exp2(sums[TOK - 1 : TOK, :])
     dec[...] = jnp.broadcast_to(decay, (8, 128))
+    for copy in fetch[1:]:
+        copy.wait()
     for g in range(BLOCKS):
         c = slice(128 * g, 128 * g + 128)
         pair = [jnp.broadcast_to(sums[:, h : h + 1], (TOK, 128)) for h in (2 * g, 2 * g + 1)]
@@ -470,7 +480,7 @@
     loop(0, GROUPS, output_group)
 
     def dp_out(i):
-        z = lax.rem(zed + i, DPS)
+        z = far_dp(i)
         return pltpu.make_async_remote_copy(
             src_ref=sum1, dst_ref=ar2.at[zed], send_sem=r2_s.at[0], recv_sem=r2_s.at[1],
             device_id={"dp": z}, device_id_type=MESH,
@@ -486,7 +496,7 @@
         came_all(ar1.at[pl.ds(0, CTX - 1)], r1_s.at[1])
         ar1[me] = part[:, cols(me)]
         sum1[...] = jnp.sum(ar1[...], axis=0)
-        loop(1, DPS, lambda i: dp_out(i).start())
+        loop(0, DPS - 1, lambda i: dp_out(i).start())
 
     steps_z = dot(zhi[...], onehot[...]) + dot(zlo[...], onehot[...])
     e = jnp.exp(-jnp.abs(raw))
@@ -510,7 +520,7 @@
         came_all(ar2.at[pl.ds(0, DPS - 1)], r2_s.at[1])
         ar2[zed] = sum1[...]
         tot[:, cols(me)] = jnp.sum(ar2[...], axis=0)
-        loop(1, CTX, lambda i: total_out(lax.rem(me + i, CTX)).start())
+        loop(0, CTX - 1, lambda i: total_out(far_first(i)).start())
 
     loop(CH // 256, CH // 128, input_grad)
 

time: 50.9 us -> 50.3 us (0.988)
  Pallas kernels: 50.2 us -> 49.5 us
    pallas_call x1, Pallas kernels: 49 us -> 48.4 us  [body(): pl.pallas_call(kernel, out_shape=[pltpu.VMEM(a.shape, a.dtype) for a in s...]
where the time goes in v5:
time: 50.3 us; the launch traced here: 50.2 us
  Pallas kernels  49.5 us (98%)
  between operations  0.64 us (1%)
    pallas_call x1, Pallas kernels, body(): pl.pallas_call(kernel, out_shape=[pltpu.VMEM(a.shape, a.dtype) for a in s...  48.4 us
    pallas_call x1, Pallas kernels, body(): pl.pallas_call(copy_kernel, out_shape=shapes, in_specs=[vmem] * 6, out_sp...  1.14 us

profile of v5, /device:TPU:1, one launch (start us, length us, event | category | flops | bytes accessed | tf_op | source)
XLA Modules:
  0.0 50.2 jit_solution(7226871678872088088)
XLA Ops:
  0.6 48.4 %shard_map.118 = (bf16[128,2560]{1,0:T(8,128)(2,1)S(1)}, bf16[128,2816]{1,0:T(8,128)(2,1)S(1)}, f32[40,128]{1,0:T(8,128)S(1)}, f32[4,2816]{1,0:T(4,128)S(1)}, f3...) custom-call(bf16[128,2816]{1,0:T(8,128)(2,1)} %bitcast.17, f32[40,128]{1,0:T(8,128)} %bitcast.19, f32[40,128]{1,0:T(8,128)} %bitcast.20, ...), custom_call_target="tpu_custom_call" | custom-call | tf_op jit(solution)/shard_map/pallas_call | solution.py:648
  49.1 1.1 %shard_map.119 = (bf16[128,2560]{1,0:T(8,128)(2,1)}, bf16[128,2816]{1,0:T(8,128)(2,1)}, f32[40,128]{1,0:T(8,128)}, f32[4,2816]{1,0:T(4,128)}, f32[22,128]{1,0:T(8,128)}, /*index=5*/f32[1,40]{1,0:T(1,128)}) custom-call(bf16[128,2560]{1,0:T(8,128)(2,1)S(1)} %get-tuple-element.18.refs_0_, bf16[128,2816]{1,0:T(8,128)(2,1)S(1)} %get-tuple-element.19.refs_1_, ...), custom_call_target="tpu_custom_call" | custom-call | tf_op jit(solution)/shard_map/pallas_call | solution.py:661

commit v6 on v5

--- a/solution.py
+++ b/solution.py
@@ -124,7 +124,7 @@
     fetch = [
         pltpu.make_async_copy(src, dst, in_sem.at[i])
         for i, (src, dst) in enumerate((
-            (ld_hbm, ldp.at[pl.ds(0, HEADS), :]), (raw_hbm, raw_ref), (x_hbm, xb), (cot_hbm, cot_ref),
+            (ld_hbm, ldp.at[pl.ds(0, HEADS), :]), (cot_hbm, cot_ref), (x_hbm, xb), (raw_hbm, raw_ref),
             (w_hbm, w_ref), (b_hbm, b_ref), (skip_hbm, skip_ref),
         ))
     ]
@@ -149,8 +149,7 @@
     sums = sums_t.T
     decay = jnp.exp2(sums[TOK - 1 : TOK, :])
     dec[...] = jnp.broadcast_to(decay, (8, 128))
-    for copy in fetch[1:]:
-        copy.wait()
+    fetch[1].wait()
     for g in range(BLOCKS):
         c = slice(128 * g, 128 * g + 128)
         pair = [jnp.broadcast_to(sums[:, h : h + 1], (TOK, 128)) for h in (2 * g, 2 * g + 1)]
@@ -206,6 +205,8 @@
         ends(g)
         scaled(g, ROWS, TOK - ROWS)
 
+    for copy in fetch[2:]:
+        copy.wait()
     loop(BLOCKS, BLOCKS + 2, later_rows)
 
     pl.semaphore_wait(barrier, CTX - 1 + DPS - 1)

time: 50.3 us -> 50.3 us (level)
  no operation moved by 1% of the time
where the time goes in v6:
time: 50.3 us; the launch traced here: 50.2 us
  Pallas kernels  49.5 us (98%)
  between operations  0.64 us (1%)
    pallas_call x1, Pallas kernels, body(): pl.pallas_call(kernel, out_shape=[pltpu.VMEM(a.shape, a.dtype) for a in s...  48.4 us
    pallas_call x1, Pallas kernels, body(): pl.pallas_call(copy_kernel, out_shape=shapes, in_specs=[vmem] * 6, out_sp...  1.14 us

profile of v6, /device:TPU:1, one launch (start us, length us, event | category | flops | bytes accessed | tf_op | source)
XLA Modules:
  0.0 50.2 jit_solution(9181354854406928547)
XLA Ops:
  0.6 48.4 %shard_map.118 = (bf16[128,2560]{1,0:T(8,128)(2,1)S(1)}, bf16[128,2816]{1,0:T(8,128)(2,1)S(1)}, f32[40,128]{1,0:T(8,128)S(1)}, f32[4,2816]{1,0:T(4,128)S(1)}, f3...) custom-call(bf16[128,2816]{1,0:T(8,128)(2,1)} %bitcast.17, f32[40,128]{1,0:T(8,128)} %bitcast.19, f32[40,128]{1,0:T(8,128)} %bitcast.20, ...), custom_call_target="tpu_custom_call" | custom-call | tf_op jit(solution)/shard_map/pallas_call | solution.py:649
  49.1 1.1 %shard_map.119 = (bf16[128,2560]{1,0:T(8,128)(2,1)}, bf16[128,2816]{1,0:T(8,128)(2,1)}, f32[40,128]{1,0:T(8,128)}, f32[4,2816]{1,0:T(4,128)}, f32[22,128]{1,0:T(8,128)}, /*index=5*/f32[1,40]{1,0:T(1,128)}) custom-call(bf16[128,2560]{1,0:T(8,128)(2,1)S(1)} %get-tuple-element.18.refs_0_, bf16[128,2816]{1,0:T(8,128)(2,1)S(1)} %get-tuple-element.19.refs_1_, ...), custom_call_target="tpu_custom_call" | custom-call | tf_op jit(solution)/shard_map/pallas_call | solution.py:662
